TPU v7x, 256 devices: a whole 4x4x8 slice. The times are simulated.
256 devices in a mesh: enc: 4 (over z_hi), ctx: 32 (over y, z_lo, x), tp: 2 (over core).
Axes of the slice: x: 4, y: 4, z: 8 (z_hi: 4, z_lo: 2; z = z_hi * 2 + z_lo), core: 2. Of those that a mesh axis runs over, the one named last changes fastest.
Arguments:
- hidden: bfloat16 [8192, 5120], P('ctx'), may hold values from -6 to 6
- deepstack: bfloat16 [4096, 5120], P(('enc', 'ctx'), 'tp'), may hold values from -6 to 6
- visual_positions: int32 [4096], replicated, may hold values from 0 to 8191, as said below
- position_ids: int32 [3, 8192], P(None, 'ctx'), may hold values from 0 to 8191
- segment_ids: int32 [8192], replicated, may hold values from 0 to 7, never falling along the last dimension, each value on 1 to 6144 neighbouring positions
- norm_gain: float32 [5120], replicated, may hold values from 0.1 to 1.9
- w_query: bfloat16 [5120, 8192], P('ctx', ('enc', 'tp')), may hold values from -0.078125 to 0.078125
- w_key: bfloat16 [5120, 1024], P('ctx', ('enc', 'tp')), may hold values from -0.078125 to 0.078125
- w_value: bfloat16 [5120, 1024], P('ctx', ('enc', 'tp')), may hold values from -0.078125 to 0.078125
- q_gain: float32 [128], replicated, may hold values from 0.5 to 12
- k_gain: float32 [128], replicated, may hold values from 0.5 to 12
Outputs:
- attended: bfloat16 [8192, 8192], P('ctx', ('enc', 'tp'))
Inputs may be any that keep to these rules, and one draw needn't show every extreme that they name: `visual_positions`: distinct positions. Owner of a position = position // 256. The 32 rows of one encoder device (aligned blocks of 32 rows) go to 16 owners, exactly 2 rows to each; every owner receives 256 // 2 visual rows.
All inputs are finite; a program needn't handle non-finite values.
Results may differ from a plain program's by a relative error of at most 0.04.
The roundings to bfloat16 on the way count: a program that leaves them out, or rounds other values in their place, can miss the bound.
Values may be sent and summed in bfloat16 or wider, within the bound.
No kernel may reach another device: no remote copies, remote signals or barrier semaphores. Data moves between devices by JAX's collectives and lax.ppermute only.
A program may use at most 64 MiB of HBM per device.

v0:
```python
import jax
import jax.numpy as jnp
from jax import lax
from jax.sharding import PartitionSpec as P

EPSILON = 1e-06
THETA = 5000000.0


def rms_scale(values):
    return lax.rsqrt(jnp.mean(values * values, axis=-1, keepdims=True) + EPSILON)


def angle_table(position_ids, head_size):
    half_size = head_size // 2
    limit = half_size - head_size // 32
    pair_index = jnp.arange(half_size, dtype=jnp.int32)
    frequency = jnp.power(jnp.float32(THETA), -2.0 * pair_index.astype(jnp.float32) / head_size)
    axis_of = jnp.where(pair_index < limit, pair_index % 3, 0)
    pair_positions = position_ids[axis_of]
    return pair_positions.T.astype(jnp.float32) * frequency[None, :]


def rotate(values, angles):
    half_size = values.shape[-1] // 2
    cosine = jnp.cos(angles)[:, None, :]
    sine_table = jnp.sin(angles)[:, None, :]
    first_half = values[..., :half_size]
    second = values[..., half_size:]
    return jnp.concatenate(
        [first_half * cosine - second * sine_table, second * cosine + first_half * sine_table],
        axis=-1,
    )


def heads_norm_rope(projected, gain, angles, head_count, head_size):
    row_count = projected.shape[0]
    values = projected.reshape(row_count, head_count, head_size)
    values = values * rms_scale(values) * gain
    return rotate(values, angles).astype(jnp.bfloat16)


def sender_slots(owners, owner_count, capacity):
    onehot = (owners[:, None] == jnp.arange(owner_count, dtype=jnp.int32)[None, :]).astype(
        jnp.int32
    )
    before = jnp.cumsum(onehot, axis=0) - onehot
    rank_in = jnp.sum(before * onehot, axis=1)
    return owners * capacity + rank_in


def on_device(
    hidden,
    deepstack,
    visual_positions,
    position_ids,
    segment_ids,
    norm_gain,
    w_query,
    w_key,
    w_value,
    q_gain,
    k_gain,
):
    tok_rows = hidden.shape[0]
    ctx_count = lax.axis_size("ctx")
    ctx_index = lax.axis_index("ctx")
    source_index = lax.axis_index(("enc", "ctx"))
    vis_rows = deepstack.shape[0]
    capacity = 2 * vis_rows // ctx_count
    own_positions = lax.dynamic_slice_in_dim(visual_positions, source_index * vis_rows, vis_rows)
    slot_of = sender_slots(own_positions // tok_rows, ctx_count, capacity)
    slot_table = (
        jnp.arange(ctx_count * capacity, dtype=jnp.int32)[:, None] == slot_of[None, :]
    ).astype(jnp.bfloat16)
    outgoing = jnp.dot(slot_table, deepstack, preferred_element_type=jnp.float32).astype(
        jnp.bfloat16
    )
    arrived = lax.all_to_all(outgoing, "ctx", split_axis=0, concat_axis=0, tiled=True)
    arrived = lax.all_gather(arrived, "enc", axis=0, tiled=True)
    arrived = lax.all_gather(arrived, "tp", axis=1, tiled=True)
    all_positions = visual_positions.reshape(-1, vis_rows)
    hits = (all_positions // tok_rows == ctx_index).astype(jnp.int32)
    hit_rank = jnp.cumsum(hits, axis=1) - hits
    local_rows = all_positions % tok_rows
    matches = (hit_rank[:, :, None] == jnp.arange(capacity, dtype=jnp.int32)[None, None, :]).astype(
        jnp.int32
    ) * hits[:, :, None]
    row_of_slot = jnp.sum(matches * local_rows[:, :, None], axis=1).reshape(-1)
    filled = jnp.sum(matches, axis=1).reshape(-1)
    scatter_table = (
        (row_of_slot[None, :] == jnp.arange(tok_rows, dtype=jnp.int32)[:, None])
        & (filled[None, :] > 0)
    ).astype(jnp.bfloat16)
    injection = jnp.dot(scatter_table, arrived, preferred_element_type=jnp.float32)
    injected = (hidden.astype(jnp.float32) + injection).astype(jnp.bfloat16)
    widened = injected.astype(jnp.float32)
    normed = (widened * rms_scale(widened) * norm_gain).astype(jnp.bfloat16)
    pieces = (
        lax.all_gather(w_query, "ctx", axis=0, tiled=True),
        lax.all_gather(w_key, "ctx", axis=0, tiled=True),
        lax.all_gather(w_value, "ctx", axis=0, tiled=True),
    )
    query, key_proj, value_proj = tuple(
        (jnp.dot(normed, piece, preferred_element_type=jnp.float32) for piece in pieces)
    )
    head_size = q_gain.shape[0]
    q_heads = w_query.shape[1] // head_size
    kv_heads = w_key.shape[1] // head_size
    group_size = q_heads // kv_heads
    angles = angle_table(position_ids, head_size)
    queries = heads_norm_rope(query, q_gain, angles, q_heads, head_size)
    keys = heads_norm_rope(key_proj, k_gain, angles, kv_heads, head_size).reshape(
        tok_rows, kv_heads * head_size
    )
    values = value_proj.astype(jnp.bfloat16)
    q_grouped = queries.reshape(tok_rows, kv_heads, group_size, head_size).transpose(1, 2, 0, 3)
    first_query = ctx_index * tok_rows
    query_pos = first_query + jnp.arange(tok_rows, dtype=jnp.int32)
    query_seg = lax.dynamic_slice_in_dim(segment_ids, first_query, tok_rows)
    factor = 1.0 / head_size**0.5

    def attend_block(state, key_block, value_block, key_first):
        count = key_block.shape[0]
        key_heads = key_block.reshape(count, kv_heads, head_size)
        value_heads = value_block.reshape(count, kv_heads, head_size)
        scores = (
            jnp.einsum("hgtd,nhd->hgtn", q_grouped, key_heads, preferred_element_type=jnp.float32)
            * factor
        )
        key_pos = key_first + jnp.arange(count, dtype=jnp.int32)
        key_seg = lax.dynamic_slice_in_dim(segment_ids, key_first, count)
        allowed = (query_pos[:, None] >= key_pos[None, :]) & (
            query_seg[:, None] == key_seg[None, :]
        )
        masked = jnp.where(allowed, scores, -1e30)
        best, row_total, accum = state
        new_best = jnp.maximum(best, jnp.max(masked, axis=-1))
        rescale = jnp.exp(best - new_best)
        weights = jnp.where(allowed, jnp.exp(masked - new_best[..., None]), 0.0)
        row_total = row_total * rescale + jnp.sum(weights, axis=-1)
        update = jnp.einsum(
            "hgtn,nhd->hgtd",
            weights.astype(jnp.bfloat16),
            value_heads,
            preferred_element_type=jnp.float32,
        )
        accum = accum * rescale[..., None] + update
        return (new_best, row_total, accum)

    def visit(state, key_block, value_block, key_first):
        return attend_block(state, key_block, value_block, key_first)

    initial = (
        jnp.full((kv_heads, group_size, tok_rows), -1e30, jnp.float32),
        jnp.zeros((kv_heads, group_size, tok_rows), jnp.float32),
        jnp.zeros((kv_heads, group_size, tok_rows, head_size), jnp.float32),
    )
    state = initial
    pieces = (
        lax.all_gather(keys, "ctx", axis=0, tiled=True),
        lax.all_gather(values, "ctx", axis=0, tiled=True),
    )
    count = pieces[0].shape[0]
    block_count = count // 512
    key_stack = pieces[0].reshape(block_count, 512, pieces[0].shape[1])
    value_stack = pieces[1].reshape(block_count, 512, pieces[1].shape[1])

    def step_block(inner, items):
        key_block, value_block, block_index = items
        return (visit(inner, key_block, value_block, block_index * 512), None)

    state, unused = lax.scan(
        step_block, state, (key_stack, value_stack, jnp.arange(block_count, dtype=jnp.int32))
    )
    best, row_total, accum = state
    attended = (accum / row_total[..., None]).astype(jnp.bfloat16)
    return attended.transpose(2, 0, 1, 3).reshape(tok_rows, q_heads * head_size)


def solution(mesh):
    placed = (
        P("ctx", None),
        P(("enc", "ctx"), "tp"),
        P(),
        P(None, "ctx"),
        P(),
        P(),
        P("ctx", ("enc", "tp")),
        P("ctx", ("enc", "tp")),
        P("ctx", ("enc", "tp")),
        P(),
        P(),
    )
    return jax.shard_map(
        on_device, mesh=mesh, in_specs=placed, out_specs=P("ctx", ("enc", "tp")), check_vma=False
    )
```

profile of v0, /device:TPU:88, one launch (start us, length us, event | category | flops | bytes accessed | tf_op | source)
XLA Modules:
  0.0 1033.6 jit_solution(8185754416457909399)
XLA Ops:
  9.0 16.3 %all_to_all.12 = bf16[32,2,2560]{2,1,0:T(2,128)(2,1)S(1)} all-to-all(bf16[32,2,2560]{2,1,0:T(2,128)(2,1)S(1)} %all_to_all.8), channel_id=1, replica_groups=mesh['enc'=4,'ctx'=32,'tp'=2] {'ctx'}, dimensions={0} | all-to-all | bytes 655360 | tf_op jit(solution)/shard_map/all_to_all | solution.py:79
  26.2 37.9 %all-gather.8.cloned.1.call-done = bf16[256,2560]{1,0:T(8,128)(2,1)} async-done(((bf16[64,2560]{1,0:T(8,128)(2,1)}), bf16[256,2560]{1,0:T(8,128)(2,1)}) %all-gather.8.cloned.1.call-update) | async-done | bytes 1310736 | tf_op jit(solution)/shard_map/all_gather | solution.py:80
  67.0 13.8 %all-gather.10.cloned.1.call-done = bf16[256,5120]{1,0:T(8,128)(2,1)} async-done(((bf16[256,2560]{1,0:T(8,128)(2,1)}), bf16[256,5120]{1,0:T(8,128)(2,1)}) %all-gather.10.cloned.1.call-update) | async-done | bytes 2621456 | tf_op jit(solution)/shard_map/all_gather | solution.py:81
  80.9 4.4 fusion.27
  85.3 145.2 %all-gather.12.cloned.1.call-done = bf16[5120,128]{1,0:T(8,128)(2,1)} async-done(((bf16[160,128]{1,0:T(8,128)(2,1)}), bf16[5120,128]{1,0:T(8,128)(2,1)}) %all-gather.12.cloned.1.call-update) | async-done | bytes 1310736 | tf_op jit(solution)/shard_map/all_gather | solution.py:101
  230.6 3.3 multiply_reduce_fusion.1
  235.7 150.4 %all-gather.18.cloned.1.call-done = bf16[5120,128]{1,0:T(8,128)(2,1)} async-done(((bf16[160,128]{1,0:T(8,128)(2,1)}), bf16[5120,128]{1,0:T(8,128)(2,1)}) %all-gather.18.cloned.1.call-update) | async-done | bytes 1310736 | tf_op jit(solution)/shard_map/all_gather | solution.py:102
  386.1 3.0 convolution_convert_fusion.1
  391.7 130.0 %all-gather.14.cloned.1.call-done = bf16[8192,128]{0,1:T(8,128)(2,1)} async-done(((bf16[256,128]{0,1:T(8,128)(2,1)}), bf16[8192,128]{0,1:T(8,128)(2,1)}) %all-gather.14.cloned.1.call-update) | async-done | bytes 2097168 | tf_op jit(solution)/shard_map/all_gather | solution.py:161
  521.7 3.2 copy.75
  524.9 162.7 %all-gather.16.cloned.1.call-done = bf16[5120,1024]{1,0:T(8,128)(2,1)} async-done(((bf16[160,1024]{1,0:T(8,128)(2,1)}), bf16[5120,1024]{1,0:T(8,128)(2,1)}) %all-gather.16.cloned.1.call-update) | async-done | bytes 10485776 | tf_op jit(solution)/shard_map/all_gather | solution.py:100
  687.6 6.5 fusion.57
  696.8 149.6 %all-gather.20.cloned.1.call-done = bf16[8192,128]{1,0:T(8,128)(2,1)} async-done(((bf16[256,128]{1,0:T(8,128)(2,1)}), bf16[8192,128]{1,0:T(8,128)(2,1)}) %all-gather.20.cloned.1.call-update) | async-done | bytes 2097168 | tf_op jit(solution)/shard_map/all_gather | solution.py:162
  846.4 177.6 %while.15 = (s32[]{:T(128)}, f32[1,8,256]{2,1,0:T(8,128)S(1)}, f32[1,8,256]{2,1,0:T(8,128)S(1)}, f32[1,8,256,128]{3,2,1,0:T(8,128)}, s32[16]{0:T(128)S(1)}, /*in...) while((s32[]{:T(128)}, f32[1,8,256]{2,1,0:T(8,128)S(1)}, ...), condition=%wide.region_11.12_spmd.clone, body=%wide.region_8.11_spmd.clone.sunk | while | flops 551695104 | bytes 32913148 | solution.py:173
  848.6 2.7 fusion.76
  851.4 4.8 fusion.79
  862.2 5.1 fusion.79
  870.5 2.7 fusion.76
  873.3 5.1 fusion.79
  884.4 5.1 fusion.79
  895.5 5.1 fusion.79
  906.6 5.1 fusion.79
  917.8 5.1 fusion.79
  928.9 5.1 fusion.79
  940.0 5.1 fusion.79
  951.1 5.1 fusion.79
  962.2 5.1 fusion.79
  973.4 5.1 fusion.79
  984.5 5.1 fusion.79
  995.6 5.1 fusion.79
  1006.7 5.1 fusion.79
  1017.8 5.1 fusion.79
  (267 shorter events, 95.9 us)
Async XLA Ops:
  6.5 2.1 copy-start
  6.5 58.9 %copy-start.3 = (s32[4096]{0:T(1024)S(1)}, s32[4096]{0:T(1024)}, u32[]{:S(2)}) copy-start(s32[4096]{0:T(1024)} %param.15) | copy-start | bytes 49156
  6.5 59.8 %copy-start.2 = (s32[3,256]{1,0:T(4,128)S(1)}, s32[3,256]{1,0:T(4,128)}, u32[]{:S(2)}) copy-start(s32[3,256]{1,0:T(4,128)} %param.16) | copy-start | bytes 9220
  6.5 74.3 %copy-start.6 = (bf16[256,5120]{1,0:T(8,128)(2,1)S(1)}, bf16[256,5120]{1,0:T(8,128)(2,1)}, u32[]{:S(2)}) copy-start(bf16[256,5120]{1,0:T(8,128)(2,1)} %param.13) | copy-start | bytes 7864324
  6.5 57.5 %all-gather.8.cloned.1.call-start = ((), (), s32[]{:S(2)}) async-start(), calls=%async_computation.1 | async-start | bytes 1638400 | tf_op jit(solution)/shard_map/all_gather | solution.py:80
  26.1 54.7 %all-gather.10.cloned.1.call-start = ((), (), s32[]{:S(2)}) async-start(), calls=%async_computation.2 | async-start | bytes 3932160 | tf_op jit(solution)/shard_map/all_gather | solution.py:81
  64.1 166.5 %all-gather.12.cloned.1.call-start = ((), (), s32[]{:S(2)}) async-start(), calls=%async_computation.3 | async-start | bytes 1351680 | tf_op jit(solution)/shard_map/all_gather | solution.py:101
  64.8 321.3 %all-gather.18.cloned.1.call-start = ((), (), s32[]{:S(2)}) async-start(), calls=%async_computation.6 | async-start | bytes 1351680 | tf_op jit(solution)/shard_map/all_gather | solution.py:102
  65.4 456.3 %all-gather.14.cloned.1.call-start = ((), (), s32[]{:S(2)}) async-start(), calls=%async_computation.4 | async-start | bytes 2162688 | tf_op jit(solution)/shard_map/all_gather | solution.py:161
  67.0 163.5 %copy-start.7 = (f32[5120]{0:T(1024)S(1)}, f32[5120]{0:T(1024)}, u32[]{:S(2)}) copy-start(f32[5120]{0:T(1024)} %param.18) | copy-start | bytes 61444
  85.3 148.6 %copy-start.4 = (f32[128]{0:T(128)S(1)}, f32[128]{0:T(128)}, u32[]{:S(2)}) copy-start(f32[128]{0:T(128)} %param.23) | copy-start | bytes 1540
  85.3 300.8 %copy-start.8 = (bf16[256,5120]{1,0:T(8,128)(2,1)S(1)}, bf16[256,5120]{1,0:T(8,128)(2,1)}, u32[]{:S(2)}) copy-start(bf16[256,5120]{1,0:T(8,128)(2,1)} %get-tuple-element.194) | copy-start | bytes 7864324
  234.9 452.7 %all-gather.16.cloned.1.call-start = ((), (), s32[]{:S(2)}) async-start(), calls=%async_computation.5 | async-start | bytes 10813440 | tf_op jit(solution)/shard_map/all_gather | solution.py:100
  235.5 610.9 %all-gather.20.cloned.1.call-start = ((), (), s32[]{:S(2)}) async-start(), calls=%async_computation.7 | async-start | bytes 2162688 | tf_op jit(solution)/shard_map/all_gather | solution.py:162
  524.9 169.8 %copy-start.5 = (f32[128]{0:T(128)S(1)}, f32[128]{0:T(128)}, u32[]{:S(2)}) copy-start(f32[128]{0:T(128)} %param.22) | copy-start | bytes 1540
  851.4 4.8 copy-start.1
  862.2 5.1 copy-start.1
  873.3 5.1 copy-start.1
  884.4 5.1 copy-start.1
  895.5 5.1 copy-start.1
  906.6 5.1 copy-start.1
  917.8 5.1 copy-start.1
  928.9 5.1 copy-start.1
  940.0 5.1 copy-start.1
  951.1 5.1 copy-start.1
  962.2 5.1 copy-start.1
  973.4 5.1 copy-start.1
  984.5 5.1 copy-start.1
  995.6 5.1 copy-start.1
  1006.7 5.1 copy-start.1
  1017.8 5.1 copy-start.1
Sparse Core Ops, SparseCore 0:
  26.3 37.7 all-gather.7
  65.9 14.9 all-gather.9
  82.7 147.8 all-gather.11
  232.2 153.8 all-gather.17
  387.7 133.9 all-gather.13
  523.3 164.2 all-gather.15
  689.4 156.9 all-gather.19
where the time goes:
time: 1040 us; the launch traced here: 1030 us
  waiting for transfers between devices  791 us (76%)
  matrix products  142 us (14%)
  local copies, waits for them, and re-layouts  31 us (3%)
  other arithmetic  27.4 us (3%)
  blocking collectives  16.3 us (2%)
  between operations  13.8 us (1%)
  loops' own time  11.2 us (1%)
    all_gather x1, waiting for transfers between devices, on_device(): lax.all_gather(w_query, 'ctx', axis=0, tiled=True)  163 us
    all_gather x1, waiting for transfers between devices, on_device(): lax.all_gather(w_value, 'ctx', axis=0, tiled=True)  150 us
    all_gather x1, waiting for transfers between devices, on_device(): lax.all_gather(values, 'ctx', axis=0, tiled=True)  150 us
    all_gather x1, waiting for transfers between devices, on_device(): lax.all_gather(w_key, 'ctx', axis=0, tiled=True)  145 us
    all_gather x1, waiting for transfers between devices, on_device(): lax.all_gather(keys, 'ctx', axis=0, tiled=True)  130 us
    dot_general x16, matrix products, attend_block(): jnp.einsum('hgtn,nhd->hgtd', weights.astype(jnp.bfloat16), value_heads, p...  81.1 us
    dot_general x16, matrix products, attend_block(): jnp.einsum('hgtd,nhd->hgtn', q_grouped, key_heads, preferred_element_type...  43.7 us
    all_gather x1, waiting for transfers between devices, on_device(): arrived = lax.all_gather(arrived, 'enc', axis=0, tiled=True)  37.9 us
  transfers between devices with their start and end apart: 7, of which 7 were waited for; matrix products, arithmetic and copies ran while one was open for 3% of the time, Pallas kernels for 0%

commit v1 on v0

v1 whole, which is shorter than its diff:
```python
import functools

import jax
import jax.numpy as jnp
import numpy as np
from jax import lax
from jax.experimental import pallas as pl
from jax.experimental.pallas import tpu as pltpu
from jax.sharding import PartitionSpec as P

EPSILON = 1e-06
THETA = 5000000.0
NX, NZ, NY = 4, 2, 4
N_CTX = NX * NZ * NY
RELATIVE = np.array([0, -1, 1, 2], np.int32)
BLOCK = 512
VMEM_BYTES = 56 * 1024 * 1024


def flat(y, z, x, core):
    return (((y % NY) * NZ + z % NZ) * NX + x % NX) * 2 + core


def all_places():
    return [
        (y, z, x, core)
        for y in range(NY)
        for z in range(NZ)
        for x in range(NX)
        for core in range(2)
    ]


def z_pairs():
    return [(flat(y, z, x, core), flat(y, 1 - z, x, core)) for y, z, x, core in all_places()]


def ring_pairs(phase, shift):
    pairs = []
    for y, z, x, core in all_places():
        along_x = (core == 0) == (phase == 0)
        target = flat(y, z, x + shift, core) if along_x else flat(y + shift, z, x, core)
        pairs.append((flat(y, z, x, core), target))
    return pairs


def shifted(values, phase, shift):
    return lax.ppermute(values, ("ctx", "tp"), ring_pairs(phase, shift))


def gather_all(own):
    other = lax.ppermute(own, ("ctx", "tp"), z_pairs())
    pair = jnp.concatenate([own, other], axis=0)
    low = shifted(pair, 0, 1)
    high = shifted(pair, 0, -1)
    far = shifted(pair, 0, 2)
    eight = jnp.concatenate([pair, low, high, far], axis=0)
    low = shifted(eight, 1, 1)
    high = shifted(eight, 1, -1)
    far_low = shifted(low[:4], 1, 1)
    far_high = shifted(high[4:], 1, -1)
    return eight, low, high, far_low, far_high


def source_order():
    index = lax.axis_index("ctx")
    core = lax.axis_index("tp")
    y, z, x = index // (NX * NZ), (index // NX) % NZ, index % NX
    slot = np.arange(N_CTX)
    late, early, other = RELATIVE[slot // 8], RELATIVE[(slot // 2) % 4], slot % 2
    by_x = jnp.where(core == 0, early, late)
    by_y = jnp.where(core == 0, late, early)
    order = ((y + by_y + NY) % NY) * (NX * NZ) + ((z + other) % NZ) * NX + (x + by_x + NX) % NX
    return order.astype(jnp.int32)


def inject_norm_kernel(core_ref, rows_ref, hidden_ref, mine_ref, theirs_ref, gain_ref, out_ref):
    step = pl.program_id(0)
    count = hidden_ref.shape[0]
    slots = rows_ref.shape[1]
    token = step * count + lax.broadcasted_iota(jnp.int32, (count, slots), 0)
    table = jnp.where(token == rows_ref[...], 1.0, 0.0).astype(jnp.bfloat16)
    mine = jnp.dot(table, mine_ref[...], preferred_element_type=jnp.float32)
    theirs = jnp.dot(table, theirs_ref[...], preferred_element_type=jnp.float32)
    first = core_ref[0] == 0
    injection = jnp.concatenate(
        [jnp.where(first, mine, theirs), jnp.where(first, theirs, mine)], axis=1
    )
    injected = (hidden_ref[...].astype(jnp.float32) + injection).astype(jnp.bfloat16)
    widened = injected.astype(jnp.float32)
    scale = lax.rsqrt(jnp.mean(widened * widened, axis=-1, keepdims=True) + EPSILON)
    normed = widened * scale * gain_ref[...]
    width = out_ref.shape[2]
    for part in range(out_ref.shape[0]):
        out_ref[part] = normed[:, part * width : (part + 1) * width].astype(jnp.bfloat16)


def inject_norm(hidden, mine, theirs, rows, gain, parts):
    tokens, width = hidden.shape
    steps = 4
    count = tokens // steps
    whole = lambda shape: pl.BlockSpec(shape, lambda i, s: (0,) * len(shape))
    return pl.pallas_call(
        inject_norm_kernel,
        out_shape=jax.ShapeDtypeStruct((parts, tokens, width // parts), jnp.bfloat16),
        grid_spec=pltpu.PrefetchScalarGridSpec(
            num_scalar_prefetch=1,
            grid=(steps,),
            in_specs=[
                whole(rows.shape),
                pl.BlockSpec((count, width), lambda i, s: (i, 0)),
                whole(mine.shape),
                whole(theirs.shape),
                whole(gain.shape),
            ],
            out_specs=pl.BlockSpec((parts, count, width // parts), lambda i, s: (0, i, 0)),
        ),
        compiler_params=pltpu.CompilerParams(vmem_limit_bytes=VMEM_BYTES),
        name="inject_norm",
    )(lax.axis_index("tp").astype(jnp.int32).reshape(1), rows, hidden, mine, theirs, gain)


def norm_rope(values, gain, cosine, sine):
    scale = lax.rsqrt(jnp.mean(values * values, axis=-1, keepdims=True) + EPSILON)
    values = values * scale * gain
    turned = pltpu.roll(values, values.shape[1] // 2, 1)
    return (values * cosine + turned * sine).astype(jnp.bfloat16)


def project_kernel(
    blocks, roped, order_ref, normed_ref, gain_ref, cos_ref, sin_ref, *refs
):
    *piece_refs, out_ref, total_ref = refs
    step = pl.program_id(0)

    @pl.when(step == 0)
    def _():
        total_ref[...] = jnp.zeros_like(total_ref)

    first = 0
    for piece_ref, count in zip(piece_refs, blocks):

        @pl.when((step >= first) & (step < first + count))
        def _(piece_ref=piece_ref):
            total = total_ref[...]
            for part in range(4):
                total += jnp.dot(
                    normed_ref[order_ref[step * 4 + part]],
                    piece_ref[part],
                    preferred_element_type=jnp.float32,
                )
            total_ref[...] = total

        first += count

    @pl.when(step == first - 1)
    def _():
        size = gain_ref.shape[1]
        for head in range(total_ref.shape[1] // size):
            lanes = slice(head * size, (head + 1) * size)
            if head < roped:
                out_ref[:, lanes] = norm_rope(
                    total_ref[:, lanes], gain_ref[...], cos_ref[...], sin_ref[...]
                )
            else:
                out_ref[:, lanes] = total_ref[:, lanes].astype(jnp.bfloat16)


def project(normed, pieces, order, gain, cosine, sine, roped):
    tokens = normed.shape[1]
    depth, columns = pieces[0].shape[1:]
    blocks = tuple(piece.shape[0] // 4 for piece in pieces)
    whole = lambda shape: pl.BlockSpec(shape, lambda i, s: (0,) * len(shape))
    specs, first = [], 0
    for count in blocks:
        specs.append(
            pl.BlockSpec(
                (4, depth, columns),
                lambda i, s, first=first, count=count: (jnp.clip(i - first, 0, count - 1), 0, 0),
            )
        )
        first += count
    return pl.pallas_call(
        functools.partial(project_kernel, blocks, roped),
        out_shape=jax.ShapeDtypeStruct((tokens, columns), jnp.bfloat16),
        grid_spec=pltpu.PrefetchScalarGridSpec(
            num_scalar_prefetch=1,
            grid=(first,),
            in_specs=[whole(normed.shape), whole(gain.shape), whole(cosine.shape), whole(sine.shape)]
            + specs,
            out_specs=whole((tokens, columns)),
            scratch_shapes=[pltpu.VMEM((tokens, columns), jnp.float32)],
        ),
        compiler_params=pltpu.CompilerParams(vmem_limit_bytes=VMEM_BYTES),
        cost_estimate=pl.CostEstimate(
            flops=2 * tokens * depth * N_CTX * columns,
            bytes_accessed=2 * depth * N_CTX * (columns + tokens),
            transcendentals=0,
        ),
        name="project",
    )(order, normed, gain, cosine, sine, *pieces)


def attend_kernel(order_ref, plan_ref, query_ref, start_ref, *refs):
    *piece_refs, out_ref, held_ref, best_ref, total_ref, semaphores = refs
    tokens = query_ref.shape[0]
    size = held_ref.shape[2] // 2
    heads = query_ref.shape[1] // size
    scale = float(np.log2(np.e) / np.sqrt(size))

    copies, slot = [], 0
    for piece_ref in piece_refs:
        for part in range(piece_ref.shape[0]):
            source = order_ref[slot]
            copies.append(
                pltpu.make_async_copy(
                    piece_ref.at[part],
                    held_ref.at[source // 2, pl.ds((source % 2) * tokens, tokens)],
                    semaphores.at[slot],
                )
            )
            slot += 1
    for copy in copies:
        copy.start()
    best_ref[...] = jnp.full_like(best_ref, -1e6)
    total_ref[...] = jnp.zeros_like(total_ref)
    for copy in copies:
        copy.wait()

    first_query = plan_ref[0]
    ones = jnp.ones((BLOCK, size), jnp.bfloat16)

    def visit(step, masked):
        keys = held_ref[step, :, :size]
        values = jnp.concatenate([held_ref[step, :, size:], ones], axis=1)
        if masked:
            position = step * BLOCK + lax.broadcasted_iota(jnp.int32, (tokens, BLOCK), 1)
            query = first_query + lax.broadcasted_iota(jnp.int32, (tokens, BLOCK), 0)
            allowed = (position <= query) & (position >= start_ref[...])
        for head in range(heads):
            scores = lax.dot_general(
                query_ref[:, head * size : (head + 1) * size],
                keys,
                (((1,), (1,)), ((), ())),
                preferred_element_type=jnp.float32,
            )
            if masked:
                scores = jnp.where(allowed, scores, -1e30)
            best = best_ref[head][:, :1]
            new_best = jnp.maximum(best, jnp.max(scores, axis=-1, keepdims=True))
            weights = jnp.exp2((scores - new_best) * scale).astype(jnp.bfloat16)
            rescale = jnp.exp2((best - new_best) * scale)
            update = jnp.dot(weights, values, preferred_element_type=jnp.float32)
            total_ref[head] = total_ref[head] * rescale + update
            best_ref[head] = jnp.broadcast_to(new_best, best_ref.shape[1:])

    @pl.loop(plan_ref[1], plan_ref[2])
    def _(step):
        visit(step, True)

    @pl.loop(plan_ref[3], plan_ref[4])
    def _(step):
        visit(step, False)

    visit(plan_ref[4], True)

    for head in range(heads):
        result = total_ref[head][:, :size] / total_ref[head][:, size:]
        out_ref[:, head * size : (head + 1) * size] = result.astype(jnp.bfloat16)


def attend(queries, pieces, order, plan, start):
    tokens, columns = queries.shape
    size = pieces[0].shape[2] // 2
    heads = columns // size
    whole = lambda shape: pl.BlockSpec(shape, lambda i, s, t: (0,) * len(shape))
    return pl.pallas_call(
        attend_kernel,
        out_shape=jax.ShapeDtypeStruct((tokens, columns), jnp.bfloat16),
        grid_spec=pltpu.PrefetchScalarGridSpec(
            num_scalar_prefetch=2,
            grid=(1,),
            in_specs=[whole(queries.shape), whole(start.shape)]
            + [pl.BlockSpec(memory_space=pl.ANY)] * len(pieces),
            out_specs=whole((tokens, columns)),
            scratch_shapes=[
                pltpu.VMEM((N_CTX * tokens // BLOCK, BLOCK, 2 * size), jnp.bfloat16),
                pltpu.VMEM((heads, tokens, size), jnp.float32),
                pltpu.VMEM((heads, tokens, 2 * size), jnp.float32),
                pltpu.SemaphoreType.DMA((N_CTX,)),
            ],
        ),
        compiler_params=pltpu.CompilerParams(vmem_limit_bytes=VMEM_BYTES),
        cost_estimate=pl.CostEstimate(
            flops=4 * tokens * columns * N_CTX * tokens // 2,
            bytes_accessed=4 * N_CTX * tokens * size + 4 * tokens * columns,
            transcendentals=heads * tokens * N_CTX * tokens // 2,
        ),
        name="attend",
    )(order, plan, queries, start, *pieces)


def angle_table(position_ids, head_size):
    half_size = head_size // 2
    limit = half_size - head_size // 32
    pair_index = jnp.arange(half_size, dtype=jnp.int32)
    frequency = jnp.power(jnp.float32(THETA), -2.0 * pair_index.astype(jnp.float32) / head_size)
    axis_of = jnp.where(pair_index < limit, pair_index % 3, 0)[None, :]
    columns = position_ids.astype(jnp.float32).T
    pair_positions = jnp.where(
        axis_of == 0, columns[:, :1], jnp.where(axis_of == 1, columns[:, 1:2], columns[:, 2:3])
    )
    return pair_positions * frequency[None, :]


def sender_slots(owners, owner_count, capacity):
    onehot = (owners[:, None] == jnp.arange(owner_count, dtype=jnp.int32)[None, :]).astype(
        jnp.int32
    )
    before = jnp.cumsum(onehot, axis=0) - onehot
    rank_in = jnp.sum(before * onehot, axis=1)
    return owners * capacity + rank_in


def arriving_rows(visual_positions, vis_rows, tok_rows, capacity, index):
    positions = visual_positions.reshape(-1, vis_rows)
    hits = (positions // tok_rows == index).astype(jnp.int32)
    rank = jnp.cumsum(hits, axis=1) - hits
    local = positions % tok_rows
    matches = (rank[:, :, None] == jnp.arange(capacity, dtype=jnp.int32)[None, None, :]) & (
        hits[:, :, None] > 0
    )
    return jnp.sum(jnp.where(matches, local[:, :, None] + 1, 0), axis=1) - 1


def on_device(
    hidden,
    deepstack,
    visual_positions,
    position_ids,
    segment_ids,
    norm_gain,
    w_query,
    w_key,
    w_value,
    q_gain,
    k_gain,
):
    tok_rows = hidden.shape[0]
    index = lax.axis_index("ctx")
    group = lax.axis_index("enc")
    vis_rows = deepstack.shape[0]
    capacity = 2 * vis_rows // N_CTX
    head_size = q_gain.shape[0]
    order = source_order()

    w_kv = jnp.concatenate([w_key, w_value], axis=1)
    kv_pieces = gather_all(w_kv[None])
    q_pieces = gather_all(w_query[None])

    own_positions = lax.dynamic_slice_in_dim(
        visual_positions, (group * N_CTX + index) * vis_rows, vis_rows
    )
    slot_of = sender_slots(own_positions // tok_rows, N_CTX, capacity)
    slot_table = (
        jnp.arange(N_CTX * capacity, dtype=jnp.int32)[:, None] == slot_of[None, :]
    ).astype(jnp.bfloat16)
    outgoing = jnp.dot(slot_table, deepstack, preferred_element_type=jnp.float32).astype(
        jnp.bfloat16
    )
    arrived = lax.all_to_all(outgoing, "ctx", split_axis=0, concat_axis=0, tiled=True)
    n_enc = lax.axis_size("enc")
    steps = [1, n_enc - 1, 2]
    mine = jnp.concatenate(
        [arrived]
        + [
            lax.ppermute(arrived, "enc", [(e, (e + step) % n_enc) for e in range(n_enc)])
            for step in steps
        ],
        axis=0,
    )
    theirs = lax.ppermute(mine, "tp", [(0, 1), (1, 0)])
    rows = arriving_rows(visual_positions, vis_rows, tok_rows, capacity, index).reshape(n_enc, -1)
    rows = jnp.concatenate(
        [
            lax.dynamic_slice_in_dim(rows, (group + n_enc - step) % n_enc, 1, axis=0)
            for step in [0] + steps
        ],
        axis=1,
    )
    normed = inject_norm(hidden, mine, theirs, rows, norm_gain[None, :], N_CTX)

    angles = angle_table(position_ids, head_size)
    cosine, sine = jnp.cos(angles), jnp.sin(angles)
    cosine = jnp.concatenate([cosine, cosine], axis=1)
    sine = jnp.concatenate([-sine, sine], axis=1)
    keys_values = project(normed, kv_pieces, order, k_gain[None, :], cosine, sine, 1)
    held = gather_all(keys_values[None])
    queries = project(
        normed, q_pieces, order, q_gain[None, :], cosine, sine, w_query.shape[1] // head_size
    )

    first_query = index * tok_rows
    own_segments = lax.dynamic_slice_in_dim(segment_ids, first_query, tok_rows)
    start = jnp.sum(
        (segment_ids[None, :] < own_segments[:, None]).astype(jnp.int32), axis=1, keepdims=True
    )
    last_step = index * tok_rows // BLOCK
    inner = (start[tok_rows - 1, 0] + BLOCK - 1) // BLOCK
    plan = jnp.stack(
        [
            first_query,
            start[0, 0] // BLOCK,
            jnp.minimum(inner, last_step),
            jnp.minimum(inner, last_step),
            last_step,
        ]
    ).astype(jnp.int32)
    return attend(queries, held, order, plan, start)


def solution(mesh):
    placed = (
        P("ctx", None),
        P(("enc", "ctx"), "tp"),
        P(),
        P(None, "ctx"),
        P(),
        P(),
        P("ctx", ("enc", "tp")),
        P("ctx", ("enc", "tp")),
        P("ctx", ("enc", "tp")),
        P(),
        P(),
    )
    return jax.shard_map(
        on_device, mesh=mesh, in_specs=placed, out_specs=P("ctx", ("enc", "tp")), check_vma=False
    )
```

time: 1040 us -> 250 us (0.24)
  the two profiles are of different devices: /device:TPU:88 before, /device:TPU:56 now
where the time goes in v1:
time: 250 us; the launch traced here: 247 us
  waiting for transfers between devices  91.2 us (36%)
  Pallas kernels  60.9 us (24%)
  starting transfers between devices  56.3 us (23%)
  local copies, waits for them, and re-layouts  26 us (10%)
  other arithmetic  8.9 us (4%)
  between operations  3.74 us (1%)
    ppermute x21, waiting for transfers between devices, shifted(): return lax.ppermute(values, ('ctx', 'tp'), ring_pairs(phase, shift))  50.2 us
    ppermute x21, starting transfers between devices, shifted(): return lax.ppermute(values, ('ctx', 'tp'), ring_pairs(phase, shift))  34.9 us
    pallas_call x1, Pallas kernels, attend(): pl.pallas_call(attend_kernel, out_shape=jax.ShapeDtypeStruct((tokens, col...  30.7 us
    ppermute x3, waiting for transfers between devices, on_device(): lax.ppermute(arrived, 'enc', [(e, (e + step) % n_enc) for e in range(n_en...  28.6 us
    pallas_call x2, Pallas kernels, project(): pl.pallas_call(functools.partial(project_kernel, blocks, roped), out_shap...  22.5 us
    unnamed x52, local copies, waits for them, and re-layouts  14.1 us
    ppermute x3, waiting for transfers between devices, gather_all(): other = lax.ppermute(own, ('ctx', 'tp'), z_pairs())  12.4 us
    ppermute x3, starting transfers between devices, on_device(): lax.ppermute(arrived, 'enc', [(e, (e + step) % n_enc) for e in range(n_en...  10.9 us
  transfers between devices with their start and end apart: 29, of which 13 were waited for; matrix products, arithmetic and copies ran while one was open for 11% of the time, Pallas kernels for 12%

profile of v1, /device:TPU:56, one launch (start us, length us, event | category | flops | bytes accessed | tf_op | source)
XLA Modules:
  0.0 247.2 jit_solution(9562813240051129609)
XLA Ops:
  3.0 8.3 %all-to-all-start = ((bf16[32,2,2560]{2,1,0:T(2,128)(2,1)}), bf16[32,2,2560]{2,1,0:T(2,128)(2,1)S(1)}, u32[]{:S(2)}, u32[]{:S(2)}) async-start(bf16[32,2,2560]{2,1,0:T(2,128)(2,1)} %all_to_all.8), calls=%async_computation | async-start | bytes 655360 | tf_op jit(solution)/shard_map/all_to_all | solution.py:371
  12.8 1.6 collective-permute-start.12
  17.2 7.2 %collective-permute-done.12 = bf16[1,160,256]{2,1,0:T(8,128)(2,1)S(1)} collective-permute-done((bf16[1,160,256]{2,1,0:T(8,128)(2,1)S(1)}, bf16[1,160,256]{2,1,0:T(8,128)(2,1)S(1)}, u32[]{:S(2)}, u32[]{:S(2)}) %collective-permute-start.12) | collective-permute-done | bytes 81952 | tf_op jit(solution)/shard_map/ppermute | solution.py:52
  24.4 1.5 collective-permute-start.13
  26.6 1.5 collective-permute-start.5
  28.2 1.8 collective-permute-start.6
  32.3 3.4 %collective-permute-start = (bf16[64,2560]{1,0:T(8,128)(2,1)S(1)}, bf16[64,2560]{1,0:T(8,128)(2,1)S(1)}, u32[]{:S(2)}, u32[]{:S(2)}) collective-permute-start(bf16[64,2560]{1,0:T(8,128)(2,1)S(1)} %all_to_all.10), channel_id=1, source_target_pairs={{0,64},{64,128},{128,192},{192,0},{1,65},{65,129},{129,193},{193,1... | collective-permute-start | bytes 983048 | tf_op jit(solution)/shard_map/ppermute | solution.py:377
  35.7 12.2 %collective-permute-done = bf16[64,2560]{1,0:T(8,128)(2,1)S(1)} collective-permute-done((bf16[64,2560]{1,0:T(8,128)(2,1)S(1)}, bf16[64,2560]{1,0:T(8,128)(2,1)S(1)}, u32[]{:S(2)}, u32[]{:S(2)}) %collective-permute-start) | collective-permute-done | bytes 327712 | tf_op jit(solution)/shard_map/ppermute | solution.py:377
  47.9 2.5 %collective-permute-start.1 = (bf16[64,2560]{1,0:T(8,128)(2,1)S(1)}, bf16[64,2560]{1,0:T(8,128)(2,1)S(1)}, u32[]{:S(2)}, u32[]{:S(2)}) collective-permute-start(bf16[64,2560]{1,0:T(8,128)(2,1)S(1)} %all_to_all.10), channel_id=1, source_target_pairs={{0,192},{64,0},{128,64},{192,128},{1,193},{65,1},{129,65},{193,129... | collective-permute-start | bytes 983048 | tf_op jit(solution)/shard_map/ppermute | solution.py:377
  50.5 14.5 %collective-permute-done.1 = bf16[64,2560]{1,0:T(8,128)(2,1)S(1)} collective-permute-done((bf16[64,2560]{1,0:T(8,128)(2,1)S(1)}, bf16[64,2560]{1,0:T(8,128)(2,1)S(1)}, u32[]{:S(2)}, u32[]{:S(2)}) %collective-permute-start.1) | collective-permute-done | bytes 327712 | tf_op jit(solution)/shard_map/ppermute | solution.py:377
  64.9 6.4 %collective-permute-start.14 = (bf16[2,160,256]{2,1,0:T(8,128)(2,1)S(1)}, bf16[2,160,256]{2,1,0:T(8,128)(2,1)S(1)}, u32[]{:S(2)}, u32[]{:S(2)}) collective-permute-start(bf16[2,160,256]{2,1,0:T(8,128)(2,1)S(1)} %pad_maximum_fusion.2), channel_id=1, source_target_pairs={{0,6},{1,49},{2,0},{3,51},{4,2},{5,53},{6,4},{7,55},{8,14},{9,57},... | collective-permute-start | bytes 491528 | tf_op jit(solution)/shard_map/ppermute | solution.py:48
  71.4 5.0 %collective-permute-start.2 = (bf16[64,2560]{1,0:T(8,128)(2,1)S(1)}, bf16[64,2560]{1,0:T(8,128)(2,1)S(1)}, u32[]{:S(2)}, u32[]{:S(2)}) collective-permute-start(bf16[64,2560]{1,0:T(8,128)(2,1)S(1)} %all_to_all.10), channel_id=1, source_target_pairs={{0,128},{64,192},{128,0},{192,64},{1,129},{65,193},{129,1},{193,65... | collective-permute-start | bytes 983048 | tf_op jit(solution)/shard_map/ppermute | solution.py:377
  76.4 2.0 constant_dynamic-update-slice_fusion.6
  79.6 2.0 constant_dynamic-update-slice_fusion.5
  83.5 2.0 collective-permute-done.2
  87.0 2.2 collective-permute-start.16
  91.4 29.9 %collective-permute-done.16.refs_1_ = bf16[8,160,256]{2,1,0:T(8,128)(2,1)S(1)} collective-permute-done((bf16[8,160,256]{2,1,0:T(8,128)(2,1)S(1)}, bf16[8,160,256]{2,1,0:T(8,128)(2,1)S(1)}, u32[]{:S(2)}, u32[]{:S(2)}) %collective-permute-start.16) | collective-permute-done | bytes 655392 | tf_op jit(solution)/shard_map/ppermute | solution.py:48
  122.1 2.2 collective-permute-start.18
  128.6 7.8 %inject_norm.1.normed_ref = bf16[32,256,160]{2,1,0:T(8,128)(2,1)} custom-call(s32[1]{0:T(128)} %bitcast.6.core_ref, s32[1,256]{1,0:T(1,128)} %pad_add_fusion.rows_ref, bf16[256,5120]{1,0:T(8,128)(2,1)} %hidden_ref.1, bf16[256,2560]{1,0:T(8,128)(2,1)} %copy-done.3, bf16[256,2560]{1,0:T(8,128)(2,1)} %copy-done.6, f32[1,5120]{1,0:T(1,128)} %bitcast.29), custom_call_target="tpu_custom_call" | custom-call | tf_op jit(solution)/shard_map/inject_norm/pallas_call | solution.py:103
  136.4 8.4 %project.3 = bf16[256,256]{1,0:T(8,128)(2,1)} custom-call(s32[32]{0:T(128)} %fusion.11.order_ref, bf16[32,256,160]{2,1,0:T(8,128)(2,1)} %inject_norm.1.normed_ref, f32[1,128]{1,0:T(1,128)} %bitcast.35, f32[256,128]{1,0:T(8,128)} %pad_maximum_fusion.3.cos_ref, f32[256,128]{1,0:T(8,128)} %pad_maximum_fusion.4.sin_ref, bf16[8,160,256]{2,1,0:T(8,128)(2,1)} %copy-done.9, ...), custom_call_target="tpu_custom_call" | custom-call | flops 671088640 | bytes 5242880 | tf_op jit(solution)/shard_map/project/pallas_call | solution.py:183
  144.8 5.2 %collective-permute-done.20 = bf16[1,256,256]{2,1,0:T(8,128)(2,1)S(1)} collective-permute-done((bf16[1,256,256]{2,1,0:T(8,128)(2,1)}, bf16[1,256,256]{2,1,0:T(8,128)(2,1)S(1)}, u32[]{:S(2)}, u32[]{:S(2)}) %collective-permute-start.20) | collective-permute-done | bytes 131104 | tf_op jit(solution)/shard_map/ppermute | solution.py:52
  151.0 3.2 %collective-permute-start.22 = (bf16[2,256,256]{2,1,0:T(8,128)(2,1)S(1)}, bf16[2,256,256]{2,1,0:T(8,128)(2,1)S(1)}, u32[]{:S(2)}, u32[]{:S(2)}) collective-permute-start(bf16[2,256,256]{2,1,0:T(8,128)(2,1)S(1)} %pad_maximum_fusion.1), channel_id=1, source_target_pairs={{0,6},{1,49},{2,0},{3,51},{4,2},{5,53},{6,4},{7,55},{8,14},{9,57},... | collective-permute-start | bytes 786440 | tf_op jit(solution)/shard_map/ppermute | solution.py:48
  154.2 1.6 constant_dynamic-update-slice_fusion.18
  160.0 5.8 %collective-permute-done.23 = bf16[2,256,256]{2,1,0:T(8,128)(2,1)S(1)} collective-permute-done((bf16[2,256,256]{2,1,0:T(8,128)(2,1)S(1)}, bf16[2,256,256]{2,1,0:T(8,128)(2,1)S(1)}, u32[]{:S(2)}, u32[]{:S(2)}) %collective-permute-start.23) | collective-permute-done | bytes 262176 | tf_op jit(solution)/shard_map/ppermute | solution.py:48
  166.5 3.9 %collective-permute-start.24 = (bf16[8,256,256]{2,1,0:T(8,128)(2,1)}, bf16[8,256,256]{2,1,0:T(8,128)(2,1)}, u32[]{:S(2)}, u32[]{:S(2)}) collective-permute-start(bf16[8,256,256]{2,1,0:T(8,128)(2,1)} %constant_dynamic-update-slice_fusion.14.refs_0_), channel_id=1, source_target_pairs={{0,16},{1,3},{2,18},{3,5},{4,20},{5,7},{6,22},{7,1},{8,24},{9,11},... | collective-permute-start | bytes 3145736 | tf_op jit(solution)/shard_map/ppermute | solution.py:48
  171.6 3.2 %collective-permute-start.10 = (bf16[4,160,1024]{2,1,0:T(8,128)(2,1)}, bf16[4,160,1024]{2,1,0:T(8,128)(2,1)}, u32[]{:S(2)}, u32[]{:S(2)}) collective-permute-start(bf16[4,160,1024]{2,1,0:T(8,128)(2,1)} %slice.49), channel_id=1, source_target_pairs={{0,16},{1,3},{2,18},{3,5},{4,20},{5,7},{6,22},{7,1},{8,24},{9,11},... | collective-permute-start | bytes 3932168 | tf_op jit(solution)/shard_map/ppermute | solution.py:48
  177.6 5.3 %collective-permute-done.24.refs_1_ = bf16[8,256,256]{2,1,0:T(8,128)(2,1)} collective-permute-done((bf16[8,256,256]{2,1,0:T(8,128)(2,1)}, bf16[8,256,256]{2,1,0:T(8,128)(2,1)}, u32[]{:S(2)}, u32[]{:S(2)}) %collective-permute-start.24) | collective-permute-done | bytes 1048608 | tf_op jit(solution)/shard_map/ppermute | solution.py:48
  184.1 3.8 %collective-permute-start.26 = (bf16[4,256,256]{2,1,0:T(8,128)(2,1)S(1)}, bf16[4,256,256]{2,1,0:T(8,128)(2,1)S(1)}, u32[]{:S(2)}, u32[]{:S(2)}) collective-permute-start(bf16[4,256,256]{2,1,0:T(8,128)(2,1)S(1)} %slice.53), channel_id=1, source_target_pairs={{0,16},{1,3},{2,18},{3,5},{4,20},{5,7},{6,22},{7,1},{8,24},{9,11},... | collective-permute-start | bytes 1572872 | tf_op jit(solution)/shard_map/ppermute | solution.py:48
  195.4 1.7 collective-permute-done.10.refs_3_
  197.0 3.7 %collective-permute-done.11.refs_4_ = bf16[4,160,1024]{2,1,0:T(8,128)(2,1)} collective-permute-done((bf16[4,160,1024]{2,1,0:T(8,128)(2,1)}, bf16[4,160,1024]{2,1,0:T(8,128)(2,1)}, u32[]{:S(2)}, u32[]{:S(2)}) %collective-permute-start.11) | collective-permute-done | bytes 1310752 | tf_op jit(solution)/shard_map/ppermute | solution.py:48
  200.7 14.1 %project.2.query_ref = bf16[256,1024]{1,0:T(8,128)(2,1)} custom-call(s32[32]{0:T(128)} %fusion.11.order_ref, bf16[32,256,160]{2,1,0:T(8,128)(2,1)} %inject_norm.1.normed_ref, f32[1,128]{1,0:T(1,128)} %bitcast.34, f32[256,128]{1,0:T(8,128)} %pad_maximum_fusion.3.cos_ref, f32[256,128]{1,0:T(8,128)} %pad_maximum_fusion.4.sin_ref, ...), custom_call_target="tpu_custom_call" | custom-call | flops 2684354560 | bytes 13107200 | tf_op jit(solution)/shard_map/project/pallas_call | solution.py:183
  216.4 30.7 %attend.1 = bf16[256,1024]{1,0:T(8,128)(2,1)} custom-call(s32[32]{0:T(128)} %fusion.11.order_ref, s32[5]{0:T(128)} %stack.20.plan_ref, bf16[256,1024]{1,0:T(8,128)(2,1)} %project.2.query_ref, s32[256,1]{1,0:T(8,128)} %copy.31.start_ref, bf16[8,256,256]{2,1,0:T(8,128)(2,1)} %constant_dynamic-update-slice_fusion.14.refs_0_, ...), custom_call_target="tpu_custom_call" | custom-call | flops 4294967296 | bytes 5242880 | tf_op jit(solution)/shard_map/attend/pallas_call | solution.py:277
  (130 shorter events, 39.2 us)
Async XLA Ops:
  3.0 29.2 %all-to-all-start = ((bf16[32,2,2560]{2,1,0:T(2,128)(2,1)}), bf16[32,2,2560]{2,1,0:T(2,128)(2,1)S(1)}, u32[]{:S(2)}, u32[]{:S(2)}) async-start(bf16[32,2,2560]{2,1,0:T(2,128)(2,1)} %all_to_all.8), calls=%async_computation | async-start | bytes 655360 | tf_op jit(solution)/shard_map/all_to_all | solution.py:371
  11.3 15.2 %collective-permute-start.4 = (bf16[1,160,1024]{2,1,0:T(8,128)(2,1)}, bf16[1,160,1024]{2,1,0:T(8,128)(2,1)S(1)}, u32[]{:S(2)}, u32[]{:S(2)}) collective-permute-start(bf16[1,160,1024]{2,1,0:T(8,128)(2,1)} %bitcast.25), channel_id=1, source_target_pairs={{0,8},{1,9},{2,10},{3,11},{4,12},{5,13},{6,14},{7,15},{8,0},{9,1},... | collective-permute-start | bytes 983048 | tf_op jit(solution)/shard_map/ppermute | solution.py:52
  12.8 11.6 %collective-permute-start.12 = (bf16[1,160,256]{2,1,0:T(8,128)(2,1)S(1)}, bf16[1,160,256]{2,1,0:T(8,128)(2,1)S(1)}, u32[]{:S(2)}, u32[]{:S(2)}) collective-permute-start(bf16[1,160,256]{2,1,0:T(8,128)(2,1)S(1)} %maximum_bitcast_fusion), channel_id=1, source_target_pairs={{0,8},{1,9},{2,10},{3,11},{4,12},{5,13},{6,14},{7,15},{8,0},{9,1},... | collective-permute-start | bytes 245768 | tf_op jit(solution)/shard_map/ppermute | solution.py:52
  24.4 61.1 %collective-permute-start.13 = (bf16[2,160,256]{2,1,0:T(8,128)(2,1)S(1)}, bf16[2,160,256]{2,1,0:T(8,128)(2,1)S(1)}, u32[]{:S(2)}, u32[]{:S(2)}) collective-permute-start(bf16[2,160,256]{2,1,0:T(8,128)(2,1)S(1)} %pad_maximum_fusion.2), channel_id=1, source_target_pairs={{0,2},{1,17},{2,4},{3,19},{4,6},{5,21},{6,0},{7,23},{8,10},{9,25},... | collective-permute-start | bytes 491528 | tf_op jit(solution)/shard_map/ppermute | solution.py:48
  26.6 44.7 %collective-permute-start.5 = (bf16[2,160,1024]{2,1,0:T(8,128)(2,1)S(1)}, bf16[2,160,1024]{2,1,0:T(8,128)(2,1)}, u32[]{:S(2)}, u32[]{:S(2)}) collective-permute-start(bf16[2,160,1024]{2,1,0:T(8,128)(2,1)S(1)} %pad_maximum_fusion), channel_id=1, source_target_pairs={{0,2},{1,17},{2,4},{3,19},{4,6},{5,21},{6,0},{7,23},{8,10},{9,25},... | collective-permute-start | bytes 1966088 | tf_op jit(solution)/shard_map/ppermute | solution.py:48
  28.2 50.2 %collective-permute-start.6 = (bf16[2,160,1024]{2,1,0:T(8,128)(2,1)S(1)}, bf16[2,160,1024]{2,1,0:T(8,128)(2,1)}, u32[]{:S(2)}, u32[]{:S(2)}) collective-permute-start(bf16[2,160,1024]{2,1,0:T(8,128)(2,1)S(1)} %pad_maximum_fusion), channel_id=1, source_target_pairs={{0,6},{1,49},{2,0},{3,51},{4,2},{5,53},{6,4},{7,55},{8,14},{9,57},... | collective-permute-start | bytes 1966088 | tf_op jit(solution)/shard_map/ppermute | solution.py:48
  29.9 51.6 %collective-permute-start.7 = (bf16[2,160,1024]{2,1,0:T(8,128)(2,1)S(1)}, bf16[2,160,1024]{2,1,0:T(8,128)(2,1)S(1)}, u32[]{:S(2)}, u32[]{:S(2)}) collective-permute-start(bf16[2,160,1024]{2,1,0:T(8,128)(2,1)S(1)} %pad_maximum_fusion), channel_id=1, source_target_pairs={{0,4},{1,33},{2,6},{3,35},{4,0},{5,37},{6,2},{7,39},{8,12},{9,41},... | collective-permute-start | bytes 1966088 | tf_op jit(solution)/shard_map/ppermute | solution.py:48
  32.3 15.6 %collective-permute-start = (bf16[64,2560]{1,0:T(8,128)(2,1)S(1)}, bf16[64,2560]{1,0:T(8,128)(2,1)S(1)}, u32[]{:S(2)}, u32[]{:S(2)}) collective-permute-start(bf16[64,2560]{1,0:T(8,128)(2,1)S(1)} %all_to_all.10), channel_id=1, source_target_pairs={{0,64},{64,128},{128,192},{192,0},{1,65},{65,129},{129,193},{193,1... | collective-permute-start | bytes 983048 | tf_op jit(solution)/shard_map/ppermute | solution.py:377
  47.9 17.0 %collective-permute-start.1 = (bf16[64,2560]{1,0:T(8,128)(2,1)S(1)}, bf16[64,2560]{1,0:T(8,128)(2,1)S(1)}, u32[]{:S(2)}, u32[]{:S(2)}) collective-permute-start(bf16[64,2560]{1,0:T(8,128)(2,1)S(1)} %all_to_all.10), channel_id=1, source_target_pairs={{0,192},{64,0},{128,64},{192,128},{1,193},{65,1},{129,65},{193,129... | collective-permute-start | bytes 983048 | tf_op jit(solution)/shard_map/ppermute | solution.py:377
  64.9 20.7 %collective-permute-start.14 = (bf16[2,160,256]{2,1,0:T(8,128)(2,1)S(1)}, bf16[2,160,256]{2,1,0:T(8,128)(2,1)S(1)}, u32[]{:S(2)}, u32[]{:S(2)}) collective-permute-start(bf16[2,160,256]{2,1,0:T(8,128)(2,1)S(1)} %pad_maximum_fusion.2), channel_id=1, source_target_pairs={{0,6},{1,49},{2,0},{3,51},{4,2},{5,53},{6,4},{7,55},{8,14},{9,57},... | collective-permute-start | bytes 491528 | tf_op jit(solution)/shard_map/ppermute | solution.py:48
  71.4 14.1 %collective-permute-start.2 = (bf16[64,2560]{1,0:T(8,128)(2,1)S(1)}, bf16[64,2560]{1,0:T(8,128)(2,1)S(1)}, u32[]{:S(2)}, u32[]{:S(2)}) collective-permute-start(bf16[64,2560]{1,0:T(8,128)(2,1)S(1)} %all_to_all.10), channel_id=1, source_target_pairs={{0,128},{64,192},{128,0},{192,64},{1,129},{65,193},{129,1},{193,65... | collective-permute-start | bytes 983048 | tf_op jit(solution)/shard_map/ppermute | solution.py:377
  78.4 8.6 %collective-permute-start.15 = (bf16[2,160,256]{2,1,0:T(8,128)(2,1)S(1)}, bf16[2,160,256]{2,1,0:T(8,128)(2,1)S(1)}, u32[]{:S(2)}, u32[]{:S(2)}) collective-permute-start(bf16[2,160,256]{2,1,0:T(8,128)(2,1)S(1)} %pad_maximum_fusion.2), channel_id=1, source_target_pairs={{0,4},{1,33},{2,6},{3,35},{4,0},{5,37},{6,2},{7,39},{8,12},{9,41},... | collective-permute-start | bytes 491528 | tf_op jit(solution)/shard_map/ppermute | solution.py:48
  81.5 45.5 %copy-start.14 = (s32[32]{0:T(128)S(1)}, s32[32]{0:T(128)}, u32[]{:S(2)}) copy-start(s32[32]{0:T(128)} %constant.212.clone) | copy-start | bytes 388
  81.5 45.5 %copy-start.15 = (s32[32]{0:T(128)S(1)}, s32[32]{0:T(128)}, u32[]{:S(2)}) copy-start(s32[32]{0:T(128)} %constant.211.clone) | copy-start | bytes 388
  81.5 45.5 %copy-start.16 = (s32[32]{0:T(128)S(1)}, s32[32]{0:T(128)}, u32[]{:S(2)}) copy-start(s32[32]{0:T(128)} %constant.210.clone) | copy-start | bytes 388
  82.4 87.9 %collective-permute-start.8 = (bf16[8,160,1024]{2,1,0:T(8,128)(2,1)}, bf16[8,160,1024]{2,1,0:T(8,128)(2,1)S(1)}, u32[]{:S(2)}, u32[]{:S(2)}) collective-permute-start(bf16[8,160,1024]{2,1,0:T(8,128)(2,1)} %constant_dynamic-update-slice_fusion.4.refs_0_), channel_id=1, source_target_pairs={{0,16},{1,3},{2,18},{3,5},{4,20},{5,7},{6,22},{7,1},{8,24},{9,11},... | collective-permute-start | bytes 7864328 | tf_op jit(solution)/shard_map/ppermute | solution.py:48
  85.4 89.4 %collective-permute-start.9 = (bf16[8,160,1024]{2,1,0:T(8,128)(2,1)}, bf16[8,160,1024]{2,1,0:T(8,128)(2,1)S(1)}, u32[]{:S(2)}, u32[]{:S(2)}) collective-permute-start(bf16[8,160,1024]{2,1,0:T(8,128)(2,1)} %constant_dynamic-update-slice_fusion.4.refs_0_), channel_id=1, source_target_pairs={{0,48},{1,7},{2,50},{3,1},{4,52},{5,3},{6,54},{7,5},{8,56},{9,15},... | collective-permute-start | bytes 7864328 | tf_op jit(solution)/shard_map/ppermute | solution.py:48
  85.5 42.0 %collective-permute-start.3 = (bf16[256,2560]{1,0:T(8,128)(2,1)S(1)}, bf16[256,2560]{1,0:T(8,128)(2,1)S(1)}, u32[]{:S(2)}, u32[]{:S(2)}) collective-permute-start(bf16[256,2560]{1,0:T(8,128)(2,1)S(1)} %constant_dynamic-update-slice_fusion.mine_ref), channel_id=1, source_target_pairs={{0,1},{1,0},{2,3},{3,2},{4,5},{5,4},{6,7},{7,6},{8,9},{9,8},{10,11... | collective-permute-start | bytes 3932168 | tf_op jit(solution)/shard_map/ppermute | solution.py:382
  87.0 34.3 %collective-permute-start.16 = (bf16[8,160,256]{2,1,0:T(8,128)(2,1)S(1)}, bf16[8,160,256]{2,1,0:T(8,128)(2,1)S(1)}, u32[]{:S(2)}, u32[]{:S(2)}) collective-permute-start(bf16[8,160,256]{2,1,0:T(8,128)(2,1)S(1)} %constant_dynamic-update-slice_fusion.9.refs_0_), channel_id=1, source_target_pairs={{0,16},{1,3},{2,18},{3,5},{4,20},{5,7},{6,22},{7,1},{8,24},{9,11},... | collective-permute-start | bytes 1966088 | tf_op jit(solution)/shard_map/ppermute | solution.py:48
  89.2 36.3 %collective-permute-start.17 = (bf16[8,160,256]{2,1,0:T(8,128)(2,1)S(1)}, bf16[8,160,256]{2,1,0:T(8,128)(2,1)S(1)}, u32[]{:S(2)}, u32[]{:S(2)}) collective-permute-start(bf16[8,160,256]{2,1,0:T(8,128)(2,1)S(1)} %constant_dynamic-update-slice_fusion.9.refs_0_), channel_id=1, source_target_pairs={{0,48},{1,7},{2,50},{3,1},{4,52},{5,3},{6,54},{7,5},{8,56},{9,15},... | collective-permute-start | bytes 1966088 | tf_op jit(solution)/shard_map/ppermute | solution.py:48
  122.1 14.2 %collective-permute-start.18 = (bf16[4,160,256]{2,1,0:T(8,128)(2,1)}, bf16[4,160,256]{2,1,0:T(8,128)(2,1)}, u32[]{:S(2)}, u32[]{:S(2)}) collective-permute-start(bf16[4,160,256]{2,1,0:T(8,128)(2,1)} %slice.51), channel_id=1, source_target_pairs={{0,16},{1,3},{2,18},{3,5},{4,20},{5,7},{6,22},{7,1},{8,24},{9,11},... | collective-permute-start | bytes 983048 | tf_op jit(solution)/shard_map/ppermute | solution.py:48
  126.3 10.0 %collective-permute-start.19 = (bf16[4,160,256]{2,1,0:T(8,128)(2,1)}, bf16[4,160,256]{2,1,0:T(8,128)(2,1)}, u32[]{:S(2)}, u32[]{:S(2)}) collective-permute-start(bf16[4,160,256]{2,1,0:T(8,128)(2,1)} %slice.52), channel_id=1, source_target_pairs={{0,48},{1,7},{2,50},{3,1},{4,52},{5,3},{6,54},{7,5},{8,56},{9,15},... | collective-permute-start | bytes 983048 | tf_op jit(solution)/shard_map/ppermute | solution.py:48
  144.8 5.2 %collective-permute-start.20 = (bf16[1,256,256]{2,1,0:T(8,128)(2,1)}, bf16[1,256,256]{2,1,0:T(8,128)(2,1)S(1)}, u32[]{:S(2)}, u32[]{:S(2)}) collective-permute-start(bf16[1,256,256]{2,1,0:T(8,128)(2,1)} %bitcast.27), channel_id=1, source_target_pairs={{0,8},{1,9},{2,10},{3,11},{4,12},{5,13},{6,14},{7,15},{8,0},{9,1},... | collective-permute-start | bytes 393224 | tf_op jit(solution)/shard_map/ppermute | solution.py:52
  150.9 7.7 %collective-permute-start.21 = (bf16[2,256,256]{2,1,0:T(8,128)(2,1)S(1)}, bf16[2,256,256]{2,1,0:T(8,128)(2,1)S(1)}, u32[]{:S(2)}, u32[]{:S(2)}) collective-permute-start(bf16[2,256,256]{2,1,0:T(8,128)(2,1)S(1)} %pad_maximum_fusion.1), channel_id=1, source_target_pairs={{0,2},{1,17},{2,4},{3,19},{4,6},{5,21},{6,0},{7,23},{8,10},{9,25},... | collective-permute-start | bytes 786440 | tf_op jit(solution)/shard_map/ppermute | solution.py:48
  151.0 8.3 %collective-permute-start.22 = (bf16[2,256,256]{2,1,0:T(8,128)(2,1)S(1)}, bf16[2,256,256]{2,1,0:T(8,128)(2,1)S(1)}, u32[]{:S(2)}, u32[]{:S(2)}) collective-permute-start(bf16[2,256,256]{2,1,0:T(8,128)(2,1)S(1)} %pad_maximum_fusion.1), channel_id=1, source_target_pairs={{0,6},{1,49},{2,0},{3,51},{4,2},{5,53},{6,4},{7,55},{8,14},{9,57},... | collective-permute-start | bytes 786440 | tf_op jit(solution)/shard_map/ppermute | solution.py:48
  155.7 10.1 %collective-permute-start.23 = (bf16[2,256,256]{2,1,0:T(8,128)(2,1)S(1)}, bf16[2,256,256]{2,1,0:T(8,128)(2,1)S(1)}, u32[]{:S(2)}, u32[]{:S(2)}) collective-permute-start(bf16[2,256,256]{2,1,0:T(8,128)(2,1)S(1)} %pad_maximum_fusion.1), channel_id=1, source_target_pairs={{0,4},{1,33},{2,6},{3,35},{4,0},{5,37},{6,2},{7,39},{8,12},{9,41},... | collective-permute-start | bytes 786440 | tf_op jit(solution)/shard_map/ppermute | solution.py:48
  166.5 16.5 %collective-permute-start.24 = (bf16[8,256,256]{2,1,0:T(8,128)(2,1)}, bf16[8,256,256]{2,1,0:T(8,128)(2,1)}, u32[]{:S(2)}, u32[]{:S(2)}) collective-permute-start(bf16[8,256,256]{2,1,0:T(8,128)(2,1)} %constant_dynamic-update-slice_fusion.14.refs_0_), channel_id=1, source_target_pairs={{0,16},{1,3},{2,18},{3,5},{4,20},{5,7},{6,22},{7,1},{8,24},{9,11},... | collective-permute-start | bytes 3145736 | tf_op jit(solution)/shard_map/ppermute | solution.py:48
  170.4 17.5 %collective-permute-start.25 = (bf16[8,256,256]{2,1,0:T(8,128)(2,1)}, bf16[8,256,256]{2,1,0:T(8,128)(2,1)}, u32[]{:S(2)}, u32[]{:S(2)}) collective-permute-start(bf16[8,256,256]{2,1,0:T(8,128)(2,1)} %constant_dynamic-update-slice_fusion.14.refs_0_), channel_id=1, source_target_pairs={{0,48},{1,7},{2,50},{3,1},{4,52},{5,3},{6,54},{7,5},{8,56},{9,15},... | collective-permute-start | bytes 3145736 | tf_op jit(solution)/shard_map/ppermute | solution.py:48
  171.6 25.4 %collective-permute-start.10 = (bf16[4,160,1024]{2,1,0:T(8,128)(2,1)}, bf16[4,160,1024]{2,1,0:T(8,128)(2,1)}, u32[]{:S(2)}, u32[]{:S(2)}) collective-permute-start(bf16[4,160,1024]{2,1,0:T(8,128)(2,1)} %slice.49), channel_id=1, source_target_pairs={{0,16},{1,3},{2,18},{3,5},{4,20},{5,7},{6,22},{7,1},{8,24},{9,11},... | collective-permute-start | bytes 3932168 | tf_op jit(solution)/shard_map/ppermute | solution.py:48
  177.6 23.2 %collective-permute-start.11 = (bf16[4,160,1024]{2,1,0:T(8,128)(2,1)}, bf16[4,160,1024]{2,1,0:T(8,128)(2,1)}, u32[]{:S(2)}, u32[]{:S(2)}) collective-permute-start(bf16[4,160,1024]{2,1,0:T(8,128)(2,1)} %slice.50), channel_id=1, source_target_pairs={{0,48},{1,7},{2,50},{3,1},{4,52},{5,3},{6,54},{7,5},{8,56},{9,15},... | collective-permute-start | bytes 3932168 | tf_op jit(solution)/shard_map/ppermute | solution.py:48
  184.1 30.7 %collective-permute-start.26 = (bf16[4,256,256]{2,1,0:T(8,128)(2,1)S(1)}, bf16[4,256,256]{2,1,0:T(8,128)(2,1)S(1)}, u32[]{:S(2)}, u32[]{:S(2)}) collective-permute-start(bf16[4,256,256]{2,1,0:T(8,128)(2,1)S(1)} %slice.53), channel_id=1, source_target_pairs={{0,16},{1,3},{2,18},{3,5},{4,20},{5,7},{6,22},{7,1},{8,24},{9,11},... | collective-permute-start | bytes 1572872 | tf_op jit(solution)/shard_map/ppermute | solution.py:48
  188.9 25.9 %collective-permute-start.27 = (bf16[4,256,256]{2,1,0:T(8,128)(2,1)S(1)}, bf16[4,256,256]{2,1,0:T(8,128)(2,1)S(1)}, u32[]{:S(2)}, u32[]{:S(2)}) collective-permute-start(bf16[4,256,256]{2,1,0:T(8,128)(2,1)S(1)} %slice.54), channel_id=1, source_target_pairs={{0,48},{1,7},{2,50},{3,1},{4,52},{5,3},{6,54},{7,5},{8,56},{9,15},... | collective-permute-start | bytes 1572872 | tf_op jit(solution)/shard_map/ppermute | solution.py:48
  (16 other events, 234.5 us)

commit v2 on v1

v2 whole, which is shorter than its diff:
```python
import functools

import jax
import jax.numpy as jnp
import numpy as np
from jax import lax
from jax.experimental import pallas as pl
from jax.experimental.pallas import tpu as pltpu
from jax.sharding import PartitionSpec as P

EPSILON = 1e-06
THETA = 5000000.0
NX, NZ, NY = 4, 2, 4
N_CTX = NX * NZ * NY
RELATIVE = np.array([0, -1, 1, 2], np.int32)
BLOCK = 512
LANES = 128
VMEM_BYTES = 56 * 1024 * 1024


def flat(y, z, x, core):
    return (((y % NY) * NZ + z % NZ) * NX + x % NX) * 2 + core


def all_places():
    return [
        (y, z, x, core)
        for y in range(NY)
        for z in range(NZ)
        for x in range(NX)
        for core in range(2)
    ]


def z_pairs():
    return [(flat(y, z, x, core), flat(y, 1 - z, x, core)) for y, z, x, core in all_places()]


def ring_pairs(phase, shift):
    pairs = []
    for y, z, x, core in all_places():
        along_x = (core == 0) == (phase == 0)
        target = flat(y, z, x + shift, core) if along_x else flat(y + shift, z, x, core)
        pairs.append((flat(y, z, x, core), target))
    return pairs


def shifted(values, phase, shift):
    return lax.ppermute(values, ("ctx", "tp"), ring_pairs(phase, shift))


def join_kernel(rows, columns, *refs):
    part_refs, out_ref, semaphores = refs[: len(rows)], refs[-2], refs[-1]
    copies, place = [], 0
    for part_ref, (first, count) in zip(part_refs, rows):
        copies.append(
            pltpu.make_async_copy(
                part_ref.at[pl.ds(first, count), :, pl.ds(*columns)],
                out_ref.at[pl.ds(place, count)],
                semaphores.at[len(copies)],
            )
        )
        place += count
    for copy in copies:
        copy.start()
    for copy in copies:
        copy.wait()


def join(parts, after=(), columns=None, rows=None):
    columns = columns or (0, parts[0].shape[2])
    rows = rows or tuple((0, part.shape[0]) for part in parts)
    shape = (sum(count for _, count in rows), parts[0].shape[1], columns[1])
    return pl.pallas_call(
        functools.partial(join_kernel, rows, columns),
        out_shape=jax.ShapeDtypeStruct(shape, parts[0].dtype),
        in_specs=[pl.BlockSpec(memory_space=pl.ANY)] * (len(parts) + len(after)),
        out_specs=pl.BlockSpec(memory_space=pltpu.VMEM),
        scratch_shapes=[pltpu.SemaphoreType.DMA((len(parts),))],
        compiler_params=pltpu.CompilerParams(vmem_limit_bytes=VMEM_BYTES),
        cost_estimate=pl.CostEstimate(
            flops=0, bytes_accessed=4 * int(np.prod(shape)), transcendentals=0
        ),
        name="join",
    )(*parts, *after)


def pair_up(own, after=()):
    return join([own, lax.ppermute(own, ("ctx", "tp"), z_pairs())], after)


def around(blocks, phase):
    return shifted(blocks, phase, 1), shifted(blocks, phase, -1), shifted(blocks, phase, 2)


def hand_on(low, high, phase, after):
    half = low.shape[0] // 2
    low_half = join([low], after, rows=((0, half),))
    high_half = join([high], after, rows=((half, half),))
    return shifted(low_half, phase, 1), shifted(high_half, phase, -1)


def source_order():
    index = lax.axis_index("ctx")
    core = lax.axis_index("tp")
    y, z, x = index // (NX * NZ), (index // NX) % NZ, index % NX
    slot = np.arange(N_CTX)
    late, early, other = RELATIVE[slot // 8], RELATIVE[(slot // 2) % 4], slot % 2
    by_x = jnp.where(core == 0, early, late)
    by_y = jnp.where(core == 0, late, early)
    order = ((y + by_y + NY) % NY) * (NX * NZ) + ((z + other) % NZ) * NX + (x + by_x + NX) % NX
    return order.astype(jnp.int32)


def norm_rope(values, gain, cosine, sine):
    scale = lax.rsqrt(jnp.mean(values * values, axis=-1, keepdims=True) + EPSILON)
    values = values * scale * gain
    turned = pltpu.roll(values, values.shape[1] // 2, 1)
    return (values * cosine + turned * sine).astype(jnp.bfloat16)


def fetch_rows(order_ref, piece_refs, held_ref, semaphores):
    depth = piece_refs[0].shape[1]
    slot = 0
    for piece_ref in piece_refs:
        for part in range(piece_ref.shape[0]):
            source = order_ref[slot]
            pltpu.make_async_copy(
                piece_ref.at[part],
                held_ref.at[pl.ds(pl.multiple_of(source * depth, depth), depth)],
                semaphores.at[source],
            ).start()
            slot += 1


def multiply_rows(normed_ref, piece_ref, held_ref, semaphores, total_ref):
    depth = piece_ref.shape[1]
    chunk = NX * depth
    total_ref[...] = jnp.zeros_like(total_ref)

    @pl.loop(0, N_CTX // NX)
    def _(step):
        for part in range(NX):
            source = step * NX + part
            pltpu.make_async_copy(
                piece_ref.at[0],
                held_ref.at[pl.ds(pl.multiple_of(source * depth, depth), depth)],
                semaphores.at[source],
            ).wait()
        rows = pl.ds(pl.multiple_of(step * chunk, chunk), chunk)
        total_ref[...] += jnp.dot(
            normed_ref[:, rows], held_ref[rows, :], preferred_element_type=jnp.float32
        )


def inject_kernel(
    groups, order_ref, rows_ref, hidden_ref, norm_gain_ref, gain_ref, cos_ref, sin_ref, *refs
):
    gathered_ref, piece_refs, refs = refs[0], refs[1:5], refs[-7:]
    normed_ref, out_ref, slots_ref, held_ref, total_ref, semaphores, arrivals = refs
    count = slots_ref.shape[1] // groups
    copies = []
    for group in range(groups):
        for side in range(2):
            place = group * 2 + side
            copies.append(
                pltpu.make_async_copy(
                    gathered_ref.at[pl.ds(place * count, count)],
                    slots_ref.at[side, pl.ds(group * count, count)],
                    arrivals.at[place],
                )
            )
    for copy in copies:
        copy.start()
    fetch_rows(order_ref, piece_refs, held_ref, semaphores)
    tokens, width = hidden_ref.shape
    slots, half = slots_ref.shape[1:]
    token = lax.broadcasted_iota(jnp.int32, (tokens, slots), 0)
    table = jnp.where(token == rows_ref[...], 1.0, 0.0).astype(jnp.bfloat16)
    for copy in copies:
        copy.wait()
    squares = jnp.zeros((tokens, LANES), jnp.float32)
    step = 512
    for first in range(0, width, step):
        lanes = slice(first, first + step)
        injection = jnp.dot(
            table,
            slots_ref[first // half, :, first % half : first % half + step],
            preferred_element_type=jnp.float32,
        )
        injected = (hidden_ref[:, lanes].astype(jnp.float32) + injection).astype(jnp.bfloat16)
        normed_ref[:, lanes] = injected
        widened = injected.astype(jnp.float32)
        for part in range(0, step, LANES):
            squares += widened[:, part : part + LANES] * widened[:, part : part + LANES]
    scale = lax.rsqrt(jnp.sum(squares, axis=-1, keepdims=True) / width + EPSILON)
    scale = jnp.broadcast_to(scale, (tokens, LANES))
    for first in range(0, width, LANES):
        lanes = slice(first, first + LANES)
        normed_ref[:, lanes] = (
            normed_ref[:, lanes].astype(jnp.float32) * scale * norm_gain_ref[:, lanes]
        ).astype(jnp.bfloat16)

    multiply_rows(normed_ref, piece_refs[0], held_ref, semaphores, total_ref)
    size = gain_ref.shape[1]
    out_ref[:, :size] = norm_rope(
        total_ref[:, :size], gain_ref[...], cos_ref[...], sin_ref[...]
    )
    out_ref[:, size:] = total_ref[:, size:].astype(jnp.bfloat16)


def whole(shape):
    return pl.BlockSpec(shape, lambda *_: (0,) * len(shape))


def inject_and_project(hidden, gathered, rows, norm_gain, pieces, order, gain, cosine, sine, after):
    tokens, width = hidden.shape
    columns = pieces[0].shape[2]
    blocks = (rows, hidden, norm_gain, gain, cosine, sine)
    others = (gathered, *pieces, *after)
    groups = lax.axis_size("enc")
    slots = gathered.shape[0] // 2
    return pl.pallas_call(
        functools.partial(inject_kernel, groups),
        out_shape=(
            jax.ShapeDtypeStruct((tokens, width), jnp.bfloat16),
            jax.ShapeDtypeStruct((tokens, columns), jnp.bfloat16),
        ),
        grid_spec=pltpu.PrefetchScalarGridSpec(
            num_scalar_prefetch=1,
            grid=(1,),
            in_specs=[whole(block.shape) for block in blocks]
            + [pl.BlockSpec(memory_space=pl.ANY)] * len(others),
            out_specs=(whole((tokens, width)), whole((tokens, columns))),
            scratch_shapes=[
                pltpu.VMEM((2, slots, width // 2), jnp.bfloat16),
                pltpu.VMEM((width, columns), jnp.bfloat16),
                pltpu.VMEM((tokens, columns), jnp.float32),
                pltpu.SemaphoreType.DMA((N_CTX,)),
                pltpu.SemaphoreType.DMA((2 * groups,)),
            ],
        ),
        compiler_params=pltpu.CompilerParams(vmem_limit_bytes=VMEM_BYTES),
        cost_estimate=pl.CostEstimate(
            flops=4 * tokens * width * columns, bytes_accessed=6 * tokens * width, transcendentals=0
        ),
        name="inject_and_project",
    )(order, *blocks, *others)


def project_kernel(order_ref, normed_ref, gain_ref, cos_ref, sin_ref, *refs):
    *piece_refs, out_ref, held_ref, total_ref, semaphores = refs
    fetch_rows(order_ref, piece_refs, held_ref, semaphores)
    multiply_rows(normed_ref, piece_refs[0], held_ref, semaphores, total_ref)
    size = gain_ref.shape[1]
    for head in range(total_ref.shape[1] // size):
        lanes = slice(head * size, (head + 1) * size)
        out_ref[:, lanes] = norm_rope(
            total_ref[:, lanes], gain_ref[...], cos_ref[...], sin_ref[...]
        )


def project(normed, pieces, order, gain, cosine, sine):
    tokens, width = normed.shape
    columns = pieces[0].shape[2]
    blocks = (normed, gain, cosine, sine)
    return pl.pallas_call(
        project_kernel,
        out_shape=jax.ShapeDtypeStruct((tokens, columns), jnp.bfloat16),
        grid_spec=pltpu.PrefetchScalarGridSpec(
            num_scalar_prefetch=1,
            grid=(1,),
            in_specs=[whole(block.shape) for block in blocks]
            + [pl.BlockSpec(memory_space=pl.ANY)] * len(pieces),
            out_specs=whole((tokens, columns)),
            scratch_shapes=[
                pltpu.VMEM((width, columns), jnp.bfloat16),
                pltpu.VMEM((tokens, columns), jnp.float32),
                pltpu.SemaphoreType.DMA((N_CTX,)),
            ],
        ),
        compiler_params=pltpu.CompilerParams(vmem_limit_bytes=VMEM_BYTES),
        cost_estimate=pl.CostEstimate(
            flops=2 * tokens * width * columns,
            bytes_accessed=2 * width * (columns + tokens),
            transcendentals=0,
        ),
        name="project",
    )(order, normed, gain, cosine, sine, *pieces)


def attend_kernel(order_ref, plan_ref, query_ref, start_ref, *refs):
    *piece_refs, out_ref, held_ref, bias_ref, best_ref, total_ref, semaphores = refs
    tokens = query_ref.shape[0]
    size = held_ref.shape[2] // 2
    heads = query_ref.shape[1] // size
    scale = float(np.log2(np.e) / np.sqrt(size))

    first_step, last_step = plan_ref[1], plan_ref[4]
    copies, slot = [], 0
    for piece_ref in piece_refs:
        for part in range(piece_ref.shape[0]):
            source = order_ref[slot]
            copy = pltpu.make_async_copy(
                piece_ref.at[part],
                held_ref.at[source // 2, pl.ds(pl.multiple_of(source % 2 * tokens, tokens), tokens)],
                semaphores.at[slot],
            )
            copies.append(((source // 2 >= first_step) & (source // 2 <= last_step), copy))
            slot += 1
    for needed, copy in copies:
        pl.when(needed)(copy.start)
    best_ref[...] = jnp.full_like(best_ref, -1e6)
    total_ref[...] = jnp.zeros_like(total_ref)
    for needed, copy in copies:
        pl.when(needed)(copy.wait)

    first_query = plan_ref[0]
    ones = jnp.ones((BLOCK, size), jnp.bfloat16)

    def visit(step, masked):
        keys = held_ref[step, :, :size].T
        values = jnp.concatenate([held_ref[step, :, size:], ones], axis=1)
        if masked:
            position = step * BLOCK + lax.broadcasted_iota(jnp.int32, (tokens, BLOCK), 1)
            query = first_query + lax.broadcasted_iota(jnp.int32, (tokens, BLOCK), 0)
            allowed = (position <= query) & (position >= start_ref[...])
            bias_ref[...] = jnp.where(allowed, 0.0, -1e30)
        def score(head):
            scores = jnp.dot(
                query_ref[:, head * size : (head + 1) * size], keys, preferred_element_type=jnp.float32
            )
            return scores + bias_ref[...] if masked else scores

        def soft(head, scores):
            best = best_ref[head]
            new_best = jnp.maximum(
                best, jnp.broadcast_to(jnp.max(scores, axis=-1, keepdims=True), best.shape)
            )
            best_ref[head] = new_best
            weights = jnp.exp2((scores - jnp.concatenate([new_best] * (BLOCK // size), axis=1)) * scale)
            return weights.astype(jnp.bfloat16), jnp.exp2((best - new_best) * scale)

        def collect(head, weights, rescale):
            update = jnp.dot(weights, values, preferred_element_type=jnp.float32)
            total_ref[head] = total_ref[head] * jnp.concatenate([rescale, rescale], axis=1) + update

        scores = score(0)
        for head in range(heads):
            later = score(head + 1) if head + 1 < heads else None
            collect(head, *soft(head, scores))
            scores = later

    @pl.loop(first_step, plan_ref[2])
    def _(step):
        visit(step, True)

    @pl.loop(plan_ref[3], last_step)
    def _(step):
        visit(step, False)

    visit(last_step, True)

    for head in range(heads):
        result = total_ref[head][:, :size] / total_ref[head][:, size:]
        out_ref[:, head * size : (head + 1) * size] = result.astype(jnp.bfloat16)


def attend(queries, pieces, order, plan, start):
    tokens, columns = queries.shape
    size = pieces[0].shape[2] // 2
    heads = columns // size
    return pl.pallas_call(
        attend_kernel,
        out_shape=jax.ShapeDtypeStruct((tokens, columns), jnp.bfloat16),
        grid_spec=pltpu.PrefetchScalarGridSpec(
            num_scalar_prefetch=2,
            grid=(1,),
            in_specs=[whole(queries.shape), whole(start.shape)]
            + [pl.BlockSpec(memory_space=pl.ANY)] * len(pieces),
            out_specs=whole((tokens, columns)),
            scratch_shapes=[
                pltpu.VMEM((N_CTX * tokens // BLOCK, BLOCK, 2 * size), jnp.bfloat16),
                pltpu.VMEM((tokens, BLOCK), jnp.float32),
                pltpu.VMEM((heads, tokens, size), jnp.float32),
                pltpu.VMEM((heads, tokens, 2 * size), jnp.float32),
                pltpu.SemaphoreType.DMA((N_CTX,)),
            ],
        ),
        compiler_params=pltpu.CompilerParams(vmem_limit_bytes=VMEM_BYTES),
        cost_estimate=pl.CostEstimate(
            flops=4 * tokens * columns * N_CTX * tokens // 2,
            bytes_accessed=4 * N_CTX * tokens * size + 4 * tokens * columns,
            transcendentals=heads * tokens * N_CTX * tokens // 2,
        ),
        name="attend",
    )(order, plan, queries, start, *pieces)


def angle_table(position_ids, head_size):
    half_size = head_size // 2
    limit = half_size - head_size // 32
    pair_index = jnp.arange(half_size, dtype=jnp.int32)
    frequency = jnp.power(jnp.float32(THETA), -2.0 * pair_index.astype(jnp.float32) / head_size)
    axis_of = jnp.where(pair_index < limit, pair_index % 3, 0)[None, :]
    columns = position_ids.astype(jnp.float32).T
    pair_positions = jnp.where(
        axis_of == 0, columns[:, :1], jnp.where(axis_of == 1, columns[:, 1:2], columns[:, 2:3])
    )
    return pair_positions * frequency[None, :]


def sender_slots(owners, owner_count, capacity):
    onehot = (owners[:, None] == jnp.arange(owner_count, dtype=jnp.int32)[None, :]).astype(
        jnp.int32
    )
    before = jnp.cumsum(onehot, axis=0) - onehot
    rank_in = jnp.sum(before * onehot, axis=1)
    return owners * capacity + rank_in


def arriving_rows(visual_positions, vis_rows, tok_rows, capacity, index):
    positions = visual_positions.reshape(-1, vis_rows)
    hits = (positions // tok_rows == index).astype(jnp.int32)
    rank = jnp.cumsum(hits, axis=1) - hits
    local = positions % tok_rows
    matches = (rank[:, :, None] == jnp.arange(capacity, dtype=jnp.int32)[None, None, :]) & (
        hits[:, :, None] > 0
    )
    return jnp.sum(jnp.where(matches, local[:, :, None] + 1, 0), axis=1) - 1


def on_device(
    hidden,
    deepstack,
    visual_positions,
    position_ids,
    segment_ids,
    norm_gain,
    w_query,
    w_key,
    w_value,
    q_gain,
    k_gain,
):
    tok_rows = hidden.shape[0]
    index = lax.axis_index("ctx")
    group = lax.axis_index("enc")
    vis_rows = deepstack.shape[0]
    capacity = 2 * vis_rows // N_CTX
    head_size = q_gain.shape[0]
    order = source_order()

    q_columns = w_query.shape[1]
    own = jnp.concatenate([w_query, w_key, w_value], axis=1)[None]
    pair = pair_up(own)
    weights = [pair, *around(pair, 0)]

    own_positions = lax.dynamic_slice_in_dim(
        visual_positions, (group * N_CTX + index) * vis_rows, vis_rows
    )
    slot_of = sender_slots(own_positions // tok_rows, N_CTX, capacity)
    slot_table = (
        jnp.arange(N_CTX * capacity, dtype=jnp.int32)[:, None] == slot_of[None, :]
    ).astype(jnp.bfloat16)
    outgoing = jnp.dot(slot_table, deepstack, preferred_element_type=jnp.float32).astype(
        jnp.bfloat16
    )
    arrived = lax.all_to_all(outgoing, "ctx", split_axis=0, concat_axis=0, tiled=True)
    gathered = lax.all_gather(arrived, ("enc", "tp"), axis=0, tiled=True)
    rows = arriving_rows(visual_positions, vis_rows, tok_rows, capacity, index).reshape(1, -1)
    angles = angle_table(position_ids, head_size)
    cosine, sine = jnp.cos(angles), jnp.sin(angles)
    cosine = jnp.concatenate([cosine, cosine], axis=1)
    sine = jnp.concatenate([-sine, sine], axis=1)

    kv_block = join(
        weights,
        after=[cosine, sine, rows],
        columns=(q_columns, own.shape[2] - q_columns),
    )
    kv_pieces = [kv_block, *around(kv_block, 1)]
    q_block = join(weights, after=kv_pieces[1:], columns=(0, q_columns))
    q_near = [shifted(q_block, 1, 1), shifted(q_block, 1, -1)]
    normed, keys_values = inject_and_project(
        hidden, gathered, rows, norm_gain[None, :], kv_pieces, order, k_gain[None, :], cosine, sine,
        [q_block],
    )
    pair = pair_up(keys_values[None])
    block = join([pair, *around(pair, 0)], after=q_near)
    q_pieces = [q_block, *q_near, *hand_on(*q_near, 1, [block])]
    held = [block, *around(block, 1)]
    queries = project(normed, q_pieces, order, q_gain[None, :], cosine, sine)

    first_query = index * tok_rows
    own_segments = lax.dynamic_slice_in_dim(segment_ids, first_query, tok_rows)
    start = jnp.sum(
        (segment_ids[None, :] < own_segments[:, None]).astype(jnp.int32), axis=1, keepdims=True
    )
    last_step = index * tok_rows // BLOCK
    inner = (start[tok_rows - 1, 0] + BLOCK - 1) // BLOCK
    plan = jnp.stack(
        [
            first_query,
            start[0, 0] // BLOCK,
            jnp.minimum(inner, last_step),
            jnp.minimum(inner, last_step),
            last_step,
        ]
    ).astype(jnp.int32)
    return attend(queries, held, order, plan, start)


def solution(mesh):
    placed = (
        P("ctx", None),
        P(("enc", "ctx"), "tp"),
        P(),
        P(None, "ctx"),
        P(),
        P(),
        P("ctx", ("enc", "tp")),
        P("ctx", ("enc", "tp")),
        P("ctx", ("enc", "tp")),
        P(),
        P(),
    )
    return jax.shard_map(
        on_device, mesh=mesh, in_specs=placed, out_specs=P("ctx", ("enc", "tp")), check_vma=False
    )
```

time: 250 us -> 208 us (0.83)
  the two profiles are of different devices: /device:TPU:56 before, /device:TPU:88 now
where the time goes in v2:
time: 208 us; the launch traced here: 204 us
  waiting for transfers between devices  77.1 us (37%)
  Pallas kernels  61.4 us (30%)
  starting transfers between devices  31.4 us (15%)
  between operations  17.1 us (8%)
  local copies, waits for them, and re-layouts  10.4 us (5%)
  other arithmetic  6.25 us (3%)
    ppermute x16, waiting for transfers between devices, shifted(): return lax.ppermute(values, ('ctx', 'tp'), ring_pairs(phase, shift))  62.4 us
    pallas_call x1, Pallas kernels, attend(): pl.pallas_call(attend_kernel, out_shape=jax.ShapeDtypeStruct((tokens, col...  22 us
    ppermute x16, starting transfers between devices, shifted(): return lax.ppermute(values, ('ctx', 'tp'), ring_pairs(phase, shift))  20.4 us
    pallas_call x7, Pallas kernels, join(): pl.pallas_call(functools.partial(join_kernel, rows, columns), out_shape=j...  16.1 us
    pallas_call x1, Pallas kernels, project(): pl.pallas_call(project_kernel, out_shape=jax.ShapeDtypeStruct((tokens, co...  12.5 us
    pallas_call x1, Pallas kernels, inject_and_project(): pl.pallas_call(functools.partial(inject_kernel, groups), out_shape=(jax.S...  10.9 us
    ppermute x2, waiting for transfers between devices, pair_up(): return join([own, lax.ppermute(own, ('ctx', 'tp'), z_pairs())], after)  8.89 us
    all_to_all x1, starting transfers between devices, on_device(): lax.all_to_all(outgoing, 'ctx', split_axis=0, concat_axis=0, tiled=True)  8.7 us
  transfers between devices with their start and end apart: 20, of which 13 were waited for; matrix products, arithmetic and copies ran while one was open for 4% of the time, Pallas kernels for 17%

profile of v2, /device:TPU:88, one launch (start us, length us, event | category | flops | bytes accessed | tf_op | source)
XLA Modules:
  0.0 203.9 jit_solution(174090186787230003)
XLA Ops:
  9.6 8.7 %all-to-all-start = ((bf16[32,2,2560]{2,1,0:T(2,128)(2,1)}), bf16[32,2,2560]{2,1,0:T(2,128)(2,1)S(1)}, u32[]{:S(2)}, u32[]{:S(2)}) async-start(bf16[32,2,2560]{2,1,0:T(2,128)(2,1)} %all_to_all.8), calls=%async_computation | async-start | bytes 655360 | tf_op jit(solution)/shard_map/all_to_all | solution.py:469
  19.4 1.6 collective-permute-start
  21.1 5.8 %all-to-all-done = bf16[32,2,2560]{2,1,0:T(2,128)(2,1)S(1)} async-done(((bf16[32,2,2560]{2,1,0:T(2,128)(2,1)}), bf16[32,2,2560]{2,1,0:T(2,128)(2,1)S(1)}, u32[]{:S(2)}, u32[]{:S(2)}) %all-to-all-start) | async-done | bytes 327712 | tf_op jit(solution)/shard_map/all_to_all | solution.py:469
  28.0 4.3 %collective-permute-done.refs_1_ = bf16[1,160,1280]{2,1,0:T(8,128)(2,1)S(1)} collective-permute-done((bf16[1,160,1280]{2,1,0:T(8,128)(2,1)S(1)}, bf16[1,160,1280]{2,1,0:T(8,128)(2,1)S(1)}, u32[]{:S(2)}, u32[]{:S(2)}) %collective-permute-start) | collective-permute-done | bytes 409632 | tf_op jit(solution)/shard_map/ppermute | solution.py:89
  33.0 2.0 join.7.refs_0_
  35.1 1.5 collective-permute-start.1
  36.6 1.8 collective-permute-start.2
  38.4 1.8 collective-permute-start.3
  42.5 6.4 %collective-permute-done.1.refs_1_ = bf16[2,160,1280]{2,1,0:T(8,128)(2,1)S(1)} collective-permute-done((bf16[2,160,1280]{2,1,0:T(8,128)(2,1)}, bf16[2,160,1280]{2,1,0:T(8,128)(2,1)S(1)}, u32[]{:S(2)}, u32[]{:S(2)}) %collective-permute-start.1) | collective-permute-done | bytes 819232 | tf_op jit(solution)/shard_map/ppermute | solution.py:49
  48.9 8.5 %collective-permute-done.2.refs_2_ = bf16[2,160,1280]{2,1,0:T(8,128)(2,1)S(1)} collective-permute-done((bf16[2,160,1280]{2,1,0:T(8,128)(2,1)}, bf16[2,160,1280]{2,1,0:T(8,128)(2,1)S(1)}, u32[]{:S(2)}, u32[]{:S(2)}) %collective-permute-start.2) | collective-permute-done | bytes 819232 | tf_op jit(solution)/shard_map/ppermute | solution.py:49
  59.5 2.1 %join.8.refs_1_ = bf16[8,160,256]{2,1,0:T(8,128)(2,1)} custom-call(bf16[2,160,1280]{2,1,0:T(8,128)(2,1)} %join.7.refs_0_, bf16[2,160,1280]{2,1,0:T(8,128)(2,1)} %copy-done.3, bf16[2,160,1280]{2,1,0:T(8,128)(2,1)} %copy-done.4, bf16[2,160,1280]{2,1,0:T(8,128)(2,1)} %copy-done.5, f32[256,128]{1,0:T(8,128)} %get-tuple-element.19.refs_4_.cos_ref, ...), custom_call_target="tpu_custom_call" | custom-call | bytes 1310720 | tf_op jit(solution)/shard_map/join/pallas_call | solution.py:74
  62.1 1.6 collective-permute-start.5
  65.1 7.4 %collective-permute-done.4.refs_4_.refs_2_ = bf16[8,160,256]{2,1,0:T(8,128)(2,1)S(1)} collective-permute-done((bf16[8,160,256]{2,1,0:T(8,128)(2,1)}, bf16[8,160,256]{2,1,0:T(8,128)(2,1)S(1)}, u32[]{:S(2)}, u32[]{:S(2)}) %collective-permute-start.4) | collective-permute-done | bytes 655392 | tf_op jit(solution)/shard_map/ppermute | solution.py:49
  72.5 8.7 %collective-permute-done.5.refs_5_.refs_3_ = bf16[8,160,256]{2,1,0:T(8,128)(2,1)S(1)} collective-permute-done((bf16[8,160,256]{2,1,0:T(8,128)(2,1)}, bf16[8,160,256]{2,1,0:T(8,128)(2,1)S(1)}, u32[]{:S(2)}, u32[]{:S(2)}) %collective-permute-start.5) | collective-permute-done | bytes 655392 | tf_op jit(solution)/shard_map/ppermute | solution.py:49
  82.9 3.2 %join.9.refs_5_.refs_0_ = bf16[8,160,1024]{2,1,0:T(8,128)(2,1)} custom-call(bf16[2,160,1280]{2,1,0:T(8,128)(2,1)} %join.7.refs_0_, bf16[2,160,1280]{2,1,0:T(8,128)(2,1)} %copy-done.3, bf16[2,160,1280]{2,1,0:T(8,128)(2,1)} %copy-done.4, bf16[2,160,1280]{2,1,0:T(8,128)(2,1)} %copy-done.5, bf16[8,160,256]{2,1,0:T(8,128)(2,1)} %copy-done.6, ...), custom_call_target="tpu_custom_call" | custom-call | bytes 5242880 | tf_op jit(solution)/shard_map/join/pallas_call | solution.py:74
  86.4 1.8 collective-permute-start.8
  88.8 10.9 %inject_and_project.1 = (bf16[256,5120]{1,0:T(8,128)(2,1)}, bf16[256,256]{1,0:T(8,128)(2,1)}) custom-call(s32[32]{0:T(128)} %fusion.11.order_ref, s32[1,256]{1,0:T(1,128)} %sub.59.refs_6_.rows_ref, bf16[256,5120]{1,0:T(8,128)(2,1)} %hidden_ref.1, f32[1,5120]{1,0:T(1,128)} %bitcast.21, f32[1,128]{1,0:T(1,128)} %bitcast.26, ...), custom_call_target="tpu_custom_call" | custom-call | flops 1342177280 | bytes 7864320 | tf_op jit(solution)/shard_map/inject_and_project/pallas_call | solution.py:223
  100.4 4.6 %collective-permute-done.9.refs_1_ = bf16[1,256,256]{2,1,0:T(8,128)(2,1)S(1)} collective-permute-done((bf16[1,256,256]{2,1,0:T(8,128)(2,1)}, bf16[1,256,256]{2,1,0:T(8,128)(2,1)S(1)}, u32[]{:S(2)}, u32[]{:S(2)}) %collective-permute-start.9) | collective-permute-done | bytes 131104 | tf_op jit(solution)/shard_map/ppermute | solution.py:89
  105.6 1.7 join.10.refs_0_
  107.3 1.7 collective-permute-start.10
  109.0 1.8 collective-permute-start.11
  111.7 12.0 %collective-permute-done.7.refs_4_.refs_0_.refs_1_ = bf16[8,160,1024]{2,1,0:T(8,128)(2,1)S(1)} collective-permute-done((bf16[8,160,1024]{2,1,0:T(8,128)(2,1)}, bf16[8,160,1024]{2,1,0:T(8,128)(2,1)S(1)}, u32[]{:S(2)}, u32[]{:S(2)}) %collective-permute-start.7) | collective-permute-done | bytes 2621472 | tf_op jit(solution)/shard_map/ppermute | solution.py:49
  126.7 2.2 %join.11.refs_1_.refs_0_ = bf16[8,256,256]{2,1,0:T(8,128)(2,1)} custom-call(bf16[2,256,256]{2,1,0:T(8,128)(2,1)} %join.10.refs_0_, bf16[2,256,256]{2,1,0:T(8,128)(2,1)} %copy-done.12, bf16[2,256,256]{2,1,0:T(8,128)(2,1)} %copy-done.13, bf16[2,256,256]{2,1,0:T(8,128)(2,1)} %copy-done.14, bf16[8,160,1024]{2,1,0:T(8,128)(2,1)} %copy-done.1, ...), custom_call_target="tpu_custom_call" | custom-call | bytes 2097152 | tf_op jit(solution)/shard_map/join/pallas_call | solution.py:74
  128.9 2.4 %join.13 = bf16[4,160,1024]{2,1,0:T(8,128)(2,1)} custom-call(bf16[8,160,1024]{2,1,0:T(8,128)(2,1)} %collective-permute-done.8.refs_5_.refs_0_.refs_2_, bf16[8,256,256]{2,1,0:T(8,128)(2,1)} %join.11.refs_1_.refs_0_), custom_call_target="tpu_custom_call" | custom-call | bytes 2621440 | tf_op jit(solution)/shard_map/join/pallas_call | solution.py:74
  132.0 2.5 %join.12 = bf16[4,160,1024]{2,1,0:T(8,128)(2,1)} custom-call(bf16[8,160,1024]{2,1,0:T(8,128)(2,1)} %copy-done.1, bf16[8,256,256]{2,1,0:T(8,128)(2,1)} %join.11.refs_1_.refs_0_), custom_call_target="tpu_custom_call" | custom-call | bytes 2621440 | tf_op jit(solution)/shard_map/join/pallas_call | solution.py:74
  134.5 2.7 %collective-permute-start.13 = (bf16[4,160,1024]{2,1,0:T(8,128)(2,1)}, bf16[4,160,1024]{2,1,0:T(8,128)(2,1)}, u32[]{:S(2)}, u32[]{:S(2)}) collective-permute-start(bf16[4,160,1024]{2,1,0:T(8,128)(2,1)} %join.12), channel_id=1, source_target_pairs={{0,16},{1,3},{2,18},{3,5},{4,20},{5,7},{6,22},{7,1},{8,24},{9,11},... | collective-permute-start | bytes 3932168 | tf_op jit(solution)/shard_map/ppermute | solution.py:49
  137.3 1.9 collective-permute-start.16
  145.9 4.5 %collective-permute-done.14.refs_4_ = bf16[4,160,1024]{2,1,0:T(8,128)(2,1)S(1)} collective-permute-done((bf16[4,160,1024]{2,1,0:T(8,128)(2,1)}, bf16[4,160,1024]{2,1,0:T(8,128)(2,1)S(1)}, u32[]{:S(2)}, u32[]{:S(2)}) %collective-permute-start.14) | collective-permute-done | bytes 1310752 | tf_op jit(solution)/shard_map/ppermute | solution.py:49
  150.4 2.2 %collective-permute-done.13.refs_3_ = bf16[4,160,1024]{2,1,0:T(8,128)(2,1)} collective-permute-done((bf16[4,160,1024]{2,1,0:T(8,128)(2,1)}, bf16[4,160,1024]{2,1,0:T(8,128)(2,1)}, u32[]{:S(2)}, u32[]{:S(2)}) %collective-permute-start.13) | collective-permute-done | bytes 1310752 | tf_op jit(solution)/shard_map/ppermute | solution.py:49
  152.6 12.5 %project.1.query_ref = bf16[256,1024]{1,0:T(8,128)(2,1)} custom-call(s32[32]{0:T(128)} %fusion.11.order_ref, bf16[256,5120]{1,0:T(8,128)(2,1)} %get-tuple-element.7.normed_ref, f32[1,128]{1,0:T(1,128)} %bitcast.27, f32[256,128]{1,0:T(8,128)} %get-tuple-element.19.refs_4_.cos_ref, f32[256,128]{1,0:T(8,128)} %get-tuple-element.20.refs_5_.sin_ref, ...), custom_call_target="tpu_custom_call" | custom-call | flops 2684354560 | bytes 13107200 | tf_op jit(solution)/shard_map/project/pallas_call | solution.py:267
  165.1 9.9 %collective-permute-done.15.refs_1_ = bf16[8,256,256]{2,1,0:T(8,128)(2,1)} collective-permute-done((bf16[8,256,256]{2,1,0:T(8,128)(2,1)S(1)}, bf16[8,256,256]{2,1,0:T(8,128)(2,1)}, u32[]{:S(2)}, u32[]{:S(2)}) %collective-permute-start.15) | collective-permute-done | bytes 1048608 | tf_op jit(solution)/shard_map/ppermute | solution.py:49
  175.0 22.0 %attend.1 = bf16[256,1024]{1,0:T(8,128)(2,1)} custom-call(s32[32]{0:T(128)} %fusion.11.order_ref, s32[5]{0:T(128)} %stack.20.plan_ref, bf16[256,1024]{1,0:T(8,128)(2,1)} %project.1.query_ref, s32[256,1]{1,0:T(8,128)} %copy.31.start_ref, bf16[8,256,256]{2,1,0:T(8,128)(2,1)} %join.11.refs_1_.refs_0_, bf16[8,256,256]{2,1,0:T(8,128)(2,1)} %collective-permute-done.15.refs_1_, ...), custom_call_target="tpu_custom_call" | custom-call | flops 4294967296 | bytes 5242880 | tf_op jit(solution)/shard_map/attend/pallas_call | solution.py:373
  (95 shorter events, 24.1 us)
Async XLA Ops:
  6.5 1.9 copy-start
  6.5 14.4 %copy-start.17 = (s32[4096]{0:T(1024)S(1)}, s32[4096]{0:T(1024)}, u32[]{:S(2)}) copy-start(s32[4096]{0:T(1024)} %param.16) | copy-start | bytes 49156
  8.7 32.3 %copy-start.18 = (s32[3,256]{1,0:T(4,128)S(1)}, s32[3,256]{1,0:T(4,128)}, u32[]{:S(2)}) copy-start(s32[3,256]{1,0:T(4,128)} %param.17) | copy-start | bytes 9220
  9.6 17.4 %all-to-all-start = ((bf16[32,2,2560]{2,1,0:T(2,128)(2,1)}), bf16[32,2,2560]{2,1,0:T(2,128)(2,1)S(1)}, u32[]{:S(2)}, u32[]{:S(2)}) async-start(bf16[32,2,2560]{2,1,0:T(2,128)(2,1)} %all_to_all.8), calls=%async_computation | async-start | bytes 655360 | tf_op jit(solution)/shard_map/all_to_all | solution.py:469
  18.3 70.5 %all-gather.2.cloned.1.call-start = ((), (), s32[]{:S(2)}) async-start(), calls=%async_computation.1 | async-start | bytes 2949120 | tf_op jit(solution)/shard_map/all_gather | solution.py:470
  19.4 12.9 %copy-start.9 = (bf16[1,160,1280]{2,1,0:T(8,128)(2,1)}, bf16[1,160,1280]{2,1,0:T(8,128)(2,1)S(1)}, u32[]{:S(2)}) copy-start(bf16[1,160,1280]{2,1,0:T(8,128)(2,1)S(1)} %maximum_bitcast_fusion.refs_0_) | copy-start | bytes 1228804
  19.4 12.9 %collective-permute-start = (bf16[1,160,1280]{2,1,0:T(8,128)(2,1)S(1)}, bf16[1,160,1280]{2,1,0:T(8,128)(2,1)S(1)}, u32[]{:S(2)}, u32[]{:S(2)}) collective-permute-start(bf16[1,160,1280]{2,1,0:T(8,128)(2,1)S(1)} %maximum_bitcast_fusion.refs_0_), channel_id=1, source_target_pairs={{0,8},{1,9},{2,10},{3,11},{4,12},{5,13},{6,14},{7,15},{8,0},{9,1},... | collective-permute-start | bytes 1228808 | tf_op jit(solution)/shard_map/ppermute | solution.py:89
  35.1 13.8 %collective-permute-start.1 = (bf16[2,160,1280]{2,1,0:T(8,128)(2,1)}, bf16[2,160,1280]{2,1,0:T(8,128)(2,1)S(1)}, u32[]{:S(2)}, u32[]{:S(2)}) collective-permute-start(bf16[2,160,1280]{2,1,0:T(8,128)(2,1)} %join.7.refs_0_), channel_id=1, source_target_pairs={{0,2},{1,17},{2,4},{3,19},{4,6},{5,21},{6,0},{7,23},{8,10},{9,25},... | collective-permute-start | bytes 2457608 | tf_op jit(solution)/shard_map/ppermute | solution.py:49
  36.6 20.8 %collective-permute-start.2 = (bf16[2,160,1280]{2,1,0:T(8,128)(2,1)}, bf16[2,160,1280]{2,1,0:T(8,128)(2,1)S(1)}, u32[]{:S(2)}, u32[]{:S(2)}) collective-permute-start(bf16[2,160,1280]{2,1,0:T(8,128)(2,1)} %join.7.refs_0_), channel_id=1, source_target_pairs={{0,6},{1,49},{2,0},{3,51},{4,2},{5,53},{6,4},{7,55},{8,14},{9,57},... | collective-permute-start | bytes 2457608 | tf_op jit(solution)/shard_map/ppermute | solution.py:49
  38.4 20.2 %collective-permute-start.3 = (bf16[2,160,1280]{2,1,0:T(8,128)(2,1)}, bf16[2,160,1280]{2,1,0:T(8,128)(2,1)S(1)}, u32[]{:S(2)}, u32[]{:S(2)}) collective-permute-start(bf16[2,160,1280]{2,1,0:T(8,128)(2,1)} %join.7.refs_0_), channel_id=1, source_target_pairs={{0,4},{1,33},{2,6},{3,35},{4,0},{5,37},{6,2},{7,39},{8,12},{9,41},... | collective-permute-start | bytes 2457608 | tf_op jit(solution)/shard_map/ppermute | solution.py:49
  48.9 9.7 %copy-start.3 = (bf16[2,160,1280]{2,1,0:T(8,128)(2,1)}, bf16[2,160,1280]{2,1,0:T(8,128)(2,1)S(1)}, u32[]{:S(2)}) copy-start(bf16[2,160,1280]{2,1,0:T(8,128)(2,1)S(1)} %collective-permute-done.1.refs_1_) | copy-start | bytes 2457604
  61.6 26.6 %copy-start.19 = (s32[32]{0:T(128)S(1)}, s32[32]{0:T(128)}, u32[]{:S(2)}) copy-start(s32[32]{0:T(128)} %constant.188.clone) | copy-start | bytes 388
  61.6 26.6 %copy-start.20 = (s32[32]{0:T(128)S(1)}, s32[32]{0:T(128)}, u32[]{:S(2)}) copy-start(s32[32]{0:T(128)} %constant.189.clone) | copy-start | bytes 388
  61.6 26.6 %copy-start.21 = (s32[32]{0:T(128)S(1)}, s32[32]{0:T(128)}, u32[]{:S(2)}) copy-start(s32[32]{0:T(128)} %constant.190.clone) | copy-start | bytes 388
  61.6 10.9 %collective-permute-start.4 = (bf16[8,160,256]{2,1,0:T(8,128)(2,1)}, bf16[8,160,256]{2,1,0:T(8,128)(2,1)S(1)}, u32[]{:S(2)}, u32[]{:S(2)}) collective-permute-start(bf16[8,160,256]{2,1,0:T(8,128)(2,1)} %join.8.refs_1_), channel_id=1, source_target_pairs={{0,16},{1,3},{2,18},{3,5},{4,20},{5,7},{6,22},{7,1},{8,24},{9,11},... | collective-permute-start | bytes 1966088 | tf_op jit(solution)/shard_map/ppermute | solution.py:49
  62.1 19.0 %collective-permute-start.5 = (bf16[8,160,256]{2,1,0:T(8,128)(2,1)}, bf16[8,160,256]{2,1,0:T(8,128)(2,1)S(1)}, u32[]{:S(2)}, u32[]{:S(2)}) collective-permute-start(bf16[8,160,256]{2,1,0:T(8,128)(2,1)} %join.8.refs_1_), channel_id=1, source_target_pairs={{0,48},{1,7},{2,50},{3,1},{4,52},{5,3},{6,54},{7,5},{8,56},{9,15},... | collective-permute-start | bytes 1966088 | tf_op jit(solution)/shard_map/ppermute | solution.py:49
  63.7 17.4 %collective-permute-start.6 = (bf16[8,160,256]{2,1,0:T(8,128)(2,1)}, bf16[8,160,256]{2,1,0:T(8,128)(2,1)S(1)}, u32[]{:S(2)}, u32[]{:S(2)}) collective-permute-start(bf16[8,160,256]{2,1,0:T(8,128)(2,1)} %join.8.refs_1_), channel_id=1, source_target_pairs={{0,32},{1,5},{2,34},{3,7},{4,36},{5,1},{6,38},{7,3},{8,40},{9,13},... | collective-permute-start | bytes 1966088 | tf_op jit(solution)/shard_map/ppermute | solution.py:49
  72.5 8.7 %copy-start.6 = (bf16[8,160,256]{2,1,0:T(8,128)(2,1)}, bf16[8,160,256]{2,1,0:T(8,128)(2,1)S(1)}, u32[]{:S(2)}) copy-start(bf16[8,160,256]{2,1,0:T(8,128)(2,1)S(1)} %collective-permute-done.4.refs_4_.refs_2_) | copy-start | bytes 1966084
  86.1 37.6 %collective-permute-start.7 = (bf16[8,160,1024]{2,1,0:T(8,128)(2,1)}, bf16[8,160,1024]{2,1,0:T(8,128)(2,1)S(1)}, u32[]{:S(2)}, u32[]{:S(2)}) collective-permute-start(bf16[8,160,1024]{2,1,0:T(8,128)(2,1)} %join.9.refs_5_.refs_0_), channel_id=1, source_target_pairs={{0,16},{1,3},{2,18},{3,5},{4,20},{5,7},{6,22},{7,1},{8,24},{9,11},... | collective-permute-start | bytes 7864328 | tf_op jit(solution)/shard_map/ppermute | solution.py:49
  86.4 38.8 %collective-permute-start.8 = (bf16[8,160,1024]{2,1,0:T(8,128)(2,1)}, bf16[8,160,1024]{2,1,0:T(8,128)(2,1)}, u32[]{:S(2)}, u32[]{:S(2)}) collective-permute-start(bf16[8,160,1024]{2,1,0:T(8,128)(2,1)} %join.9.refs_5_.refs_0_), channel_id=1, source_target_pairs={{0,48},{1,7},{2,50},{3,1},{4,52},{5,3},{6,54},{7,5},{8,56},{9,15},... | collective-permute-start | bytes 7864328 | tf_op jit(solution)/shard_map/ppermute | solution.py:49
  99.7 5.3 %collective-permute-start.9 = (bf16[1,256,256]{2,1,0:T(8,128)(2,1)}, bf16[1,256,256]{2,1,0:T(8,128)(2,1)S(1)}, u32[]{:S(2)}, u32[]{:S(2)}) collective-permute-start(bf16[1,256,256]{2,1,0:T(8,128)(2,1)} %bitcast.19), channel_id=1, source_target_pairs={{0,8},{1,9},{2,10},{3,11},{4,12},{5,13},{6,14},{7,15},{8,0},{9,1},... | collective-permute-start | bytes 393224 | tf_op jit(solution)/shard_map/ppermute | solution.py:89
  107.3 17.9 %collective-permute-start.10 = (bf16[2,256,256]{2,1,0:T(8,128)(2,1)}, bf16[2,256,256]{2,1,0:T(8,128)(2,1)S(1)}, u32[]{:S(2)}, u32[]{:S(2)}) collective-permute-start(bf16[2,256,256]{2,1,0:T(8,128)(2,1)} %join.10.refs_0_), channel_id=1, source_target_pairs={{0,2},{1,17},{2,4},{3,19},{4,6},{5,21},{6,0},{7,23},{8,10},{9,25},... | collective-permute-start | bytes 786440 | tf_op jit(solution)/shard_map/ppermute | solution.py:49
  109.0 16.2 %collective-permute-start.11 = (bf16[2,256,256]{2,1,0:T(8,128)(2,1)}, bf16[2,256,256]{2,1,0:T(8,128)(2,1)S(1)}, u32[]{:S(2)}, u32[]{:S(2)}) collective-permute-start(bf16[2,256,256]{2,1,0:T(8,128)(2,1)} %join.10.refs_0_), channel_id=1, source_target_pairs={{0,6},{1,49},{2,0},{3,51},{4,2},{5,53},{6,4},{7,55},{8,14},{9,57},... | collective-permute-start | bytes 786440 | tf_op jit(solution)/shard_map/ppermute | solution.py:49
  110.8 14.4 %collective-permute-start.12 = (bf16[2,256,256]{2,1,0:T(8,128)(2,1)}, bf16[2,256,256]{2,1,0:T(8,128)(2,1)S(1)}, u32[]{:S(2)}, u32[]{:S(2)}) collective-permute-start(bf16[2,256,256]{2,1,0:T(8,128)(2,1)} %join.10.refs_0_), channel_id=1, source_target_pairs={{0,4},{1,33},{2,6},{3,35},{4,0},{5,37},{6,2},{7,39},{8,12},{9,41},... | collective-permute-start | bytes 786440 | tf_op jit(solution)/shard_map/ppermute | solution.py:49
  131.3 5.9 %copy-start.2 = (bf16[8,256,256]{2,1,0:T(8,128)(2,1)S(1)}, bf16[8,256,256]{2,1,0:T(8,128)(2,1)}, u32[]{:S(2)}) copy-start(bf16[8,256,256]{2,1,0:T(8,128)(2,1)} %join.11.refs_1_.refs_0_) | copy-start | bytes 3145732
  131.3 7.9 %copy-start.16 = (s32[8192]{0:T(1024)S(1)}, s32[8192]{0:T(1024)}, u32[]{:S(2)}) copy-start(s32[8192]{0:T(1024)} %param.18) | copy-start | bytes 98308
  131.3 19.1 %collective-permute-start.14 = (bf16[4,160,1024]{2,1,0:T(8,128)(2,1)}, bf16[4,160,1024]{2,1,0:T(8,128)(2,1)S(1)}, u32[]{:S(2)}, u32[]{:S(2)}) collective-permute-start(bf16[4,160,1024]{2,1,0:T(8,128)(2,1)} %join.13), channel_id=1, source_target_pairs={{0,48},{1,7},{2,50},{3,1},{4,52},{5,3},{6,54},{7,5},{8,56},{9,15},... | collective-permute-start | bytes 3932168 | tf_op jit(solution)/shard_map/ppermute | solution.py:49
  134.5 18.1 %collective-permute-start.13 = (bf16[4,160,1024]{2,1,0:T(8,128)(2,1)}, bf16[4,160,1024]{2,1,0:T(8,128)(2,1)}, u32[]{:S(2)}, u32[]{:S(2)}) collective-permute-start(bf16[4,160,1024]{2,1,0:T(8,128)(2,1)} %join.12), channel_id=1, source_target_pairs={{0,16},{1,3},{2,18},{3,5},{4,20},{5,7},{6,22},{7,1},{8,24},{9,11},... | collective-permute-start | bytes 3932168 | tf_op jit(solution)/shard_map/ppermute | solution.py:49
  137.2 37.8 %collective-permute-start.15 = (bf16[8,256,256]{2,1,0:T(8,128)(2,1)S(1)}, bf16[8,256,256]{2,1,0:T(8,128)(2,1)}, u32[]{:S(2)}, u32[]{:S(2)}) collective-permute-start(bf16[8,256,256]{2,1,0:T(8,128)(2,1)S(1)} %copy-done.2), channel_id=1, source_target_pairs={{0,16},{1,3},{2,18},{3,5},{4,20},{5,7},{6,22},{7,1},{8,24},{9,11},... | collective-permute-start | bytes 3145736 | tf_op jit(solution)/shard_map/ppermute | solution.py:49
  137.3 37.7 %collective-permute-start.16 = (bf16[8,256,256]{2,1,0:T(8,128)(2,1)S(1)}, bf16[8,256,256]{2,1,0:T(8,128)(2,1)}, u32[]{:S(2)}, u32[]{:S(2)}) collective-permute-start(bf16[8,256,256]{2,1,0:T(8,128)(2,1)S(1)} %copy-done.2), channel_id=1, source_target_pairs={{0,48},{1,7},{2,50},{3,1},{4,52},{5,3},{6,54},{7,5},{8,56},{9,15},... | collective-permute-start | bytes 3145736 | tf_op jit(solution)/shard_map/ppermute | solution.py:49
  139.2 35.8 %collective-permute-start.17 = (bf16[8,256,256]{2,1,0:T(8,128)(2,1)S(1)}, bf16[8,256,256]{2,1,0:T(8,128)(2,1)}, u32[]{:S(2)}, u32[]{:S(2)}) collective-permute-start(bf16[8,256,256]{2,1,0:T(8,128)(2,1)S(1)} %copy-done.2), channel_id=1, source_target_pairs={{0,32},{1,5},{2,34},{3,7},{4,36},{5,1},{6,38},{7,3},{8,40},{9,13},... | collective-permute-start | bytes 3145736 | tf_op jit(solution)/shard_map/ppermute | solution.py:49
  150.4 2.2 %copy-start.10 = (bf16[4,160,1024]{2,1,0:T(8,128)(2,1)}, bf16[4,160,1024]{2,1,0:T(8,128)(2,1)S(1)}, u32[]{:S(2)}) copy-start(bf16[4,160,1024]{2,1,0:T(8,128)(2,1)S(1)} %collective-permute-done.14.refs_4_) | copy-start | bytes 3932164
  (10 other events, 9.1 us)
Sparse Core Ops, SparseCore 0:
  27.9 39.5 all-gather.1

commit v3 on v2

--- a/solution.py
+++ b/solution.py
@@ -85,19 +85,27 @@
     )(*parts, *after)
 
 
-def pair_up(own, after=()):
-    return join([own, lax.ppermute(own, ("ctx", "tp"), z_pairs())], after)
+def across(blocks):
+    return lax.ppermute(blocks, ("ctx", "tp"), z_pairs())
+
+
+def nothing_kernel(*refs):
+    pass
+
+
+def hold(arrays, after):
+    return pl.pallas_call(
+        nothing_kernel,
+        out_shape=tuple(jax.ShapeDtypeStruct(array.shape, array.dtype) for array in arrays),
+        in_specs=[pl.BlockSpec(memory_space=pl.ANY)] * (len(arrays) + len(after)),
+        out_specs=(pl.BlockSpec(memory_space=pl.ANY),) * len(arrays),
+        input_output_aliases={place: place for place in range(len(arrays))},
+        name="hold",
+    )(*arrays, *after)
 
 
 def around(blocks, phase):
     return shifted(blocks, phase, 1), shifted(blocks, phase, -1), shifted(blocks, phase, 2)
-
-
-def hand_on(low, high, phase, after):
-    half = low.shape[0] // 2
-    low_half = join([low], after, rows=((0, half),))
-    high_half = join([high], after, rows=((half, half),))
-    return shifted(low_half, phase, 1), shifted(high_half, phase, -1)
 
 
 def source_order():
@@ -119,34 +127,22 @@
     return (values * cosine + turned * sine).astype(jnp.bfloat16)
 
 
-def fetch_rows(order_ref, piece_refs, held_ref, semaphores):
+def lay_rows(order_ref, piece_refs, held_ref):
     depth = piece_refs[0].shape[1]
     slot = 0
     for piece_ref in piece_refs:
         for part in range(piece_ref.shape[0]):
-            source = order_ref[slot]
-            pltpu.make_async_copy(
-                piece_ref.at[part],
-                held_ref.at[pl.ds(pl.multiple_of(source * depth, depth), depth)],
-                semaphores.at[source],
-            ).start()
+            first = pl.multiple_of(order_ref[slot] * depth, depth)
+            held_ref[pl.ds(first, depth), :] = piece_ref[part]
             slot += 1
 
 
-def multiply_rows(normed_ref, piece_ref, held_ref, semaphores, total_ref):
-    depth = piece_ref.shape[1]
-    chunk = NX * depth
+def multiply_rows(normed_ref, held_ref, total_ref):
+    chunk = 1024
     total_ref[...] = jnp.zeros_like(total_ref)
 
-    @pl.loop(0, N_CTX // NX)
+    @pl.loop(0, held_ref.shape[0] // chunk)
     def _(step):
-        for part in range(NX):
-            source = step * NX + part
-            pltpu.make_async_copy(
-                piece_ref.at[0],
-                held_ref.at[pl.ds(pl.multiple_of(source * depth, depth), depth)],
-                semaphores.at[source],
-            ).wait()
         rows = pl.ds(pl.multiple_of(step * chunk, chunk), chunk)
         total_ref[...] += jnp.dot(
             normed_ref[:, rows], held_ref[rows, :], preferred_element_type=jnp.float32
@@ -156,29 +152,18 @@
 def inject_kernel(
     groups, order_ref, rows_ref, hidden_ref, norm_gain_ref, gain_ref, cos_ref, sin_ref, *refs
 ):
-    gathered_ref, piece_refs, refs = refs[0], refs[1:5], refs[-7:]
-    normed_ref, out_ref, slots_ref, held_ref, total_ref, semaphores, arrivals = refs
+    gathered_ref, piece_refs, refs = refs[0], refs[1:5], refs[-5:]
+    normed_ref, out_ref, slots_ref, held_ref, total_ref = refs
     count = slots_ref.shape[1] // groups
-    copies = []
-    for group in range(groups):
-        for side in range(2):
-            place = group * 2 + side
-            copies.append(
-                pltpu.make_async_copy(
-                    gathered_ref.at[pl.ds(place * count, count)],
-                    slots_ref.at[side, pl.ds(group * count, count)],
-                    arrivals.at[place],
-                )
-            )
-    for copy in copies:
-        copy.start()
-    fetch_rows(order_ref, piece_refs, held_ref, semaphores)
+    for place in range(2 * groups):
+        slots_ref[place % 2, place // 2 * count : (place // 2 + 1) * count] = gathered_ref[
+            place * count : (place + 1) * count
+        ]
+    lay_rows(order_ref, piece_refs, held_ref)
     tokens, width = hidden_ref.shape
     slots, half = slots_ref.shape[1:]
     token = lax.broadcasted_iota(jnp.int32, (tokens, slots), 0)
     table = jnp.where(token == rows_ref[...], 1.0, 0.0).astype(jnp.bfloat16)
-    for copy in copies:
-        copy.wait()
     squares = jnp.zeros((tokens, LANES), jnp.float32)
     step = 512
     for first in range(0, width, step):
@@ -201,7 +186,7 @@
             normed_ref[:, lanes].astype(jnp.float32) * scale * norm_gain_ref[:, lanes]
         ).astype(jnp.bfloat16)
 
-    multiply_rows(normed_ref, piece_refs[0], held_ref, semaphores, total_ref)
+    multiply_rows(normed_ref, held_ref, total_ref)
     size = gain_ref.shape[1]
     out_ref[:, :size] = norm_rope(
         total_ref[:, :size], gain_ref[...], cos_ref[...], sin_ref[...]
@@ -217,7 +202,7 @@
     tokens, width = hidden.shape
     columns = pieces[0].shape[2]
     blocks = (rows, hidden, norm_gain, gain, cosine, sine)
-    others = (gathered, *pieces, *after)
+    others = (gathered, *pieces)
     groups = lax.axis_size("enc")
     slots = gathered.shape[0] // 2
     return pl.pallas_call(
@@ -230,14 +215,13 @@
             num_scalar_prefetch=1,
             grid=(1,),
             in_specs=[whole(block.shape) for block in blocks]
-            + [pl.BlockSpec(memory_space=pl.ANY)] * len(others),
+            + [whole(other.shape) for other in others]
+            + [pl.BlockSpec(memory_space=pl.ANY)] * len(after),
             out_specs=(whole((tokens, width)), whole((tokens, columns))),
             scratch_shapes=[
                 pltpu.VMEM((2, slots, width // 2), jnp.bfloat16),
                 pltpu.VMEM((width, columns), jnp.bfloat16),
                 pltpu.VMEM((tokens, columns), jnp.float32),
-                pltpu.SemaphoreType.DMA((N_CTX,)),
-                pltpu.SemaphoreType.DMA((2 * groups,)),
             ],
         ),
         compiler_params=pltpu.CompilerParams(vmem_limit_bytes=VMEM_BYTES),
@@ -245,13 +229,19 @@
             flops=4 * tokens * width * columns, bytes_accessed=6 * tokens * width, transcendentals=0
         ),
         name="inject_and_project",
-    )(order, *blocks, *others)
-
-
-def project_kernel(order_ref, normed_ref, gain_ref, cos_ref, sin_ref, *refs):
-    *piece_refs, out_ref, held_ref, total_ref, semaphores = refs
-    fetch_rows(order_ref, piece_refs, held_ref, semaphores)
-    multiply_rows(normed_ref, piece_refs[0], held_ref, semaphores, total_ref)
+    )(order, *blocks, *others, *after)
+
+
+def project_kernel(
+    parts, order_ref, places_ref, gain_ref, cos_ref, sin_ref, *refs
+):
+    part_refs, piece_refs, refs = refs[:parts], refs[parts:-4], refs[-4:]
+    out_ref, normed_ref, held_ref, total_ref = refs
+    for part, part_ref in enumerate(part_refs):
+        lanes = pl.ds(pl.multiple_of(places_ref[part], LANES), part_ref.shape[1])
+        normed_ref[:, lanes] = part_ref[...]
+    lay_rows(order_ref, piece_refs, held_ref)
+    multiply_rows(normed_ref, held_ref, total_ref)
     size = gain_ref.shape[1]
     for head in range(total_ref.shape[1] // size):
         lanes = slice(head * size, (head + 1) * size)
@@ -260,23 +250,25 @@
         )
 
 
-def project(normed, pieces, order, gain, cosine, sine):
-    tokens, width = normed.shape
+def project(parts, places, pieces, order, gain, cosine, sine):
+    tokens = parts[0].shape[0]
+    width = sum(part.shape[1] for part in parts)
     columns = pieces[0].shape[2]
-    blocks = (normed, gain, cosine, sine)
+    blocks = (gain, cosine, sine)
+    others = (*parts, *pieces)
     return pl.pallas_call(
-        project_kernel,
+        functools.partial(project_kernel, len(parts)),
         out_shape=jax.ShapeDtypeStruct((tokens, columns), jnp.bfloat16),
         grid_spec=pltpu.PrefetchScalarGridSpec(
-            num_scalar_prefetch=1,
+            num_scalar_prefetch=2,
             grid=(1,),
             in_specs=[whole(block.shape) for block in blocks]
-            + [pl.BlockSpec(memory_space=pl.ANY)] * len(pieces),
+            + [whole(other.shape) for other in others],
             out_specs=whole((tokens, columns)),
             scratch_shapes=[
+                pltpu.VMEM((tokens, width), jnp.bfloat16),
                 pltpu.VMEM((width, columns), jnp.bfloat16),
                 pltpu.VMEM((tokens, columns), jnp.float32),
-                pltpu.SemaphoreType.DMA((N_CTX,)),
             ],
         ),
         compiler_params=pltpu.CompilerParams(vmem_limit_bytes=VMEM_BYTES),
@@ -286,35 +278,31 @@
             transcendentals=0,
         ),
         name="project",
-    )(order, normed, gain, cosine, sine, *pieces)
-
-
-def attend_kernel(order_ref, plan_ref, query_ref, start_ref, *refs):
-    *piece_refs, out_ref, held_ref, bias_ref, best_ref, total_ref, semaphores = refs
-    tokens = query_ref.shape[0]
+    )(order, places, *blocks, *others)
+
+
+def attend_kernel(order_ref, plan_ref, near_ref, far_ref, start_ref, *refs):
+    *piece_refs, out_ref, held_ref, bias_ref, best_ref, total_ref = refs
+    tokens = near_ref.shape[0]
     size = held_ref.shape[2] // 2
-    heads = query_ref.shape[1] // size
+    half = near_ref.shape[1] // size
+    heads = 2 * half
     scale = float(np.log2(np.e) / np.sqrt(size))
 
     first_step, last_step = plan_ref[1], plan_ref[4]
-    copies, slot = [], 0
+    slot = 0
     for piece_ref in piece_refs:
         for part in range(piece_ref.shape[0]):
             source = order_ref[slot]
-            copy = pltpu.make_async_copy(
-                piece_ref.at[part],
-                held_ref.at[source // 2, pl.ds(pl.multiple_of(source % 2 * tokens, tokens), tokens)],
-                semaphores.at[slot],
-            )
-            copies.append(((source // 2 >= first_step) & (source // 2 <= last_step), copy))
+
+            @pl.when((source // 2 >= first_step) & (source // 2 <= last_step))
+            def _(source=source, part=part, piece_ref=piece_ref):
+                here = pl.ds(pl.multiple_of(source % 2 * tokens, tokens), tokens)
+                held_ref[source // 2, here, :] = piece_ref[part]
+
             slot += 1
-    for needed, copy in copies:
-        pl.when(needed)(copy.start)
     best_ref[...] = jnp.full_like(best_ref, -1e6)
     total_ref[...] = jnp.zeros_like(total_ref)
-    for needed, copy in copies:
-        pl.when(needed)(copy.wait)
-
     first_query = plan_ref[0]
     ones = jnp.ones((BLOCK, size), jnp.bfloat16)
 
@@ -327,9 +315,9 @@
             allowed = (position <= query) & (position >= start_ref[...])
             bias_ref[...] = jnp.where(allowed, 0.0, -1e30)
         def score(head):
-            scores = jnp.dot(
-                query_ref[:, head * size : (head + 1) * size], keys, preferred_element_type=jnp.float32
-            )
+            query_ref = near_ref if head < half else far_ref
+            lanes = slice(head % half * size, (head % half + 1) * size)
+            scores = jnp.dot(query_ref[:, lanes], keys, preferred_element_type=jnp.float32)
             return scores + bias_ref[...] if masked else scores
 
         def soft(head, scores):
@@ -363,11 +351,13 @@
 
     for head in range(heads):
         result = total_ref[head][:, :size] / total_ref[head][:, size:]
-        out_ref[:, head * size : (head + 1) * size] = result.astype(jnp.bfloat16)
+        first = pl.multiple_of(plan_ref[5 + head // half] + head % half * size, size)
+        out_ref[:, pl.ds(first, size)] = result.astype(jnp.bfloat16)
 
 
 def attend(queries, pieces, order, plan, start):
-    tokens, columns = queries.shape
+    tokens, columns = queries[0].shape
+    columns *= 2
     size = pieces[0].shape[2] // 2
     heads = columns // size
     return pl.pallas_call(
@@ -376,15 +366,14 @@
         grid_spec=pltpu.PrefetchScalarGridSpec(
             num_scalar_prefetch=2,
             grid=(1,),
-            in_specs=[whole(queries.shape), whole(start.shape)]
-            + [pl.BlockSpec(memory_space=pl.ANY)] * len(pieces),
+            in_specs=[whole(queries[0].shape), whole(queries[1].shape), whole(start.shape)]
+            + [whole(piece.shape) for piece in pieces],
             out_specs=whole((tokens, columns)),
             scratch_shapes=[
                 pltpu.VMEM((N_CTX * tokens // BLOCK, BLOCK, 2 * size), jnp.bfloat16),
                 pltpu.VMEM((tokens, BLOCK), jnp.float32),
                 pltpu.VMEM((heads, tokens, size), jnp.float32),
                 pltpu.VMEM((heads, tokens, 2 * size), jnp.float32),
-                pltpu.SemaphoreType.DMA((N_CTX,)),
             ],
         ),
         compiler_params=pltpu.CompilerParams(vmem_limit_bytes=VMEM_BYTES),
@@ -394,7 +383,7 @@
             transcendentals=heads * tokens * N_CTX * tokens // 2,
         ),
         name="attend",
-    )(order, plan, queries, start, *pieces)
+    )(order, plan, *queries, start, *pieces)
 
 
 def angle_table(position_ids, head_size):
@@ -451,9 +440,17 @@
     head_size = q_gain.shape[0]
     order = source_order()
 
-    q_columns = w_query.shape[1]
-    own = jnp.concatenate([w_query, w_key, w_value], axis=1)[None]
-    pair = pair_up(own)
+    core = lax.axis_index("tp")
+    side = index // NX % NZ
+    columns = w_query.shape[1] // NZ
+    w_kv = jnp.concatenate([w_key, w_value], axis=1)
+
+    def with_kv(first):
+        kept = lax.dynamic_slice_in_dim(w_query, first * columns, columns, axis=1)
+        return jnp.concatenate([kept, w_kv], axis=1)[None]
+
+    own, other = with_kv(side), across(with_kv(1 - side))
+    pair = join([own, other])
     weights = [pair, *around(pair, 0)]
 
     own_positions = lax.dynamic_slice_in_dim(
@@ -469,28 +466,40 @@
     arrived = lax.all_to_all(outgoing, "ctx", split_axis=0, concat_axis=0, tiled=True)
     gathered = lax.all_gather(arrived, ("enc", "tp"), axis=0, tiled=True)
     rows = arriving_rows(visual_positions, vis_rows, tok_rows, capacity, index).reshape(1, -1)
+
+    def tables(angles):
+        cosine, sine = jnp.cos(angles), jnp.sin(angles)
+        return jnp.concatenate([cosine, cosine], axis=1), jnp.concatenate([-sine, sine], axis=1)
+
     angles = angle_table(position_ids, head_size)
-    cosine, sine = jnp.cos(angles), jnp.sin(angles)
-    cosine = jnp.concatenate([cosine, cosine], axis=1)
-    sine = jnp.concatenate([-sine, sine], axis=1)
+    own_tables, other_tables = tables(angles), tables(across(angles))
 
     kv_block = join(
-        weights,
-        after=[cosine, sine, rows],
-        columns=(q_columns, own.shape[2] - q_columns),
+        weights, after=[*own_tables, *other_tables, rows], columns=(columns, w_kv.shape[1])
     )
     kv_pieces = [kv_block, *around(kv_block, 1)]
-    q_block = join(weights, after=kv_pieces[1:], columns=(0, q_columns))
-    q_near = [shifted(q_block, 1, 1), shifted(q_block, 1, -1)]
+    q_pieces = [*hold([join(weights[:2], columns=(0, columns)), join(weights[2:], columns=(0, columns))], kv_pieces[1:])]
+    for shift in (1, -1):
+        q_pieces += [shifted(part, 1, shift) for part in q_pieces[:2]]
     normed, keys_values = inject_and_project(
-        hidden, gathered, rows, norm_gain[None, :], kv_pieces, order, k_gain[None, :], cosine, sine,
-        [q_block],
-    )
-    pair = pair_up(keys_values[None])
-    block = join([pair, *around(pair, 0)], after=q_near)
-    q_pieces = [q_block, *q_near, *hand_on(*q_near, 1, [block])]
-    held = [block, *around(block, 1)]
-    queries = project(normed, q_pieces, order, q_gain[None, :], cosine, sine)
+        hidden, gathered, rows, norm_gain[None, :], kv_pieces, order, k_gain[None, :], *own_tables,
+        [q_pieces[0]],
+    )
+    own = keys_values[None]
+    pair = join([own, across(own)], after=q_pieces[2:])
+    q_pieces[2], q_pieces[5] = hold([q_pieces[2], q_pieces[5]], [pair])
+    q_pieces += [shifted(q_pieces[2], 1, 1), shifted(q_pieces[5], 1, -1)]
+    width = normed.shape[1] // 2
+    (half,) = hold([lax.dynamic_slice_in_dim(normed, core * width, width, axis=1)], [pair])
+    half = across(half)
+    held_block = join([pair, *around(pair, 0)], after=q_pieces[6:])
+    (half,) = hold([half], [held_block])
+    rest = lax.ppermute(half, "tp", [(0, 1), (1, 0)])
+    held = [held_block, *around(held_block, 1)]
+    places = jnp.stack([core * width, (1 - core) * width]).astype(jnp.int32)
+    gain = q_gain[None, :]
+    own_queries = project([normed], jnp.zeros(1, jnp.int32), q_pieces, order, gain, *own_tables)
+    far_queries = across(project([half, rest], places, q_pieces, order, gain, *other_tables))
 
     first_query = index * tok_rows
     own_segments = lax.dynamic_slice_in_dim(segment_ids, first_query, tok_rows)
@@ -506,9 +515,11 @@
             jnp.minimum(inner, last_step),
             jnp.minimum(inner, last_step),
             last_step,
+            side * columns,
+            (1 - side) * columns,
         ]
     ).astype(jnp.int32)
-    return attend(queries, held, order, plan, start)
+    return attend([own_queries, far_queries], held, order, plan, start)
 
 
 def solution(mesh):

time: 208 us -> 191 us (0.918)
  waiting for transfers between devices: 77.1 us -> 41.5 us
  blocking collectives: 0 us -> 16.3 us
  local copies, waits for them, and re-layouts: 10.4 us -> 16.7 us
  starting transfers between devices: 31.4 us -> 28.4 us
  Pallas kernels: 61.4 us -> 58.7 us
  other arithmetic: 6.25 us -> 8.8 us
    ppermute x16 -> x18, waiting for transfers between devices: 62.4 us -> 34 us  [shifted(): return lax.ppermute(values, ('ctx', 'tp'), ring_pairs(phase, shift))]
    all_to_all x0 -> x1, blocking collectives: none -> 16.3 us  [on_device(): lax.all_to_all(outgoing, 'ctx', split_axis=0, concat_axis=0, tiled=True)]
    all_to_all x1 -> x0, starting transfers between devices: 8.7 us -> none  [on_device(): lax.all_to_all(outgoing, 'ctx', split_axis=0, concat_axis=0, tiled=True)]
    all_to_all x1 -> x0, waiting for transfers between devices: 5.83 us -> none  [on_device(): lax.all_to_all(outgoing, 'ctx', split_axis=0, concat_axis=0, tiled=True)]
    pallas_call x7 -> x6, Pallas kernels: 16.1 us -> 11.6 us  [join(): pl.pallas_call(functools.partial(join_kernel, rows, columns), out_shape=j...]
    unnamed x44 -> x64, local copies, waits for them, and re-layouts: 5.57 us -> 9.66 us
    pallas_call x1 -> x6, Pallas kernels: 12.5 us -> 16.1 us  [the longest x2 16.1 us: project(): pl.pallas_call(functools.partial(project_kernel, len(parts)), out_shape=j...]
    ppermute x16 -> x18, starting transfers between devices: 20.4 us -> 23.4 us  [shifted(): return lax.ppermute(values, ('ctx', 'tp'), ring_pairs(phase, shift))]
  transfers between devices with their start and end apart: 20 -> 25, of which waited for: 13 -> 12; matrix products, arithmetic and copies ran while one was open for 4% -> 7% of each run, Pallas kernels for 17% -> 19%
where the time goes in v3:
time: 191 us; the launch traced here: 188 us
  Pallas kernels  58.7 us (31%)
  waiting for transfers between devices  41.5 us (22%)
  starting transfers between devices  28.4 us (15%)
  between operations  17 us (9%)
  local copies, waits for them, and re-layouts  16.7 us (9%)
  blocking collectives  16.3 us (9%)
  other arithmetic  8.8 us (5%)
    ppermute x18, waiting for transfers between devices, shifted(): return lax.ppermute(values, ('ctx', 'tp'), ring_pairs(phase, shift))  34 us
    ppermute x18, starting transfers between devices, shifted(): return lax.ppermute(values, ('ctx', 'tp'), ring_pairs(phase, shift))  23.4 us
    pallas_call x1, Pallas kernels, attend(): pl.pallas_call(attend_kernel, out_shape=jax.ShapeDtypeStruct((tokens, col...  22 us
    all_to_all x1, blocking collectives, on_device(): lax.all_to_all(outgoing, 'ctx', split_axis=0, concat_axis=0, tiled=True)  16.3 us
    pallas_call x2, Pallas kernels, project(): pl.pallas_call(functools.partial(project_kernel, len(parts)), out_shape=j...  16.1 us
    pallas_call x6, Pallas kernels, join(): pl.pallas_call(functools.partial(join_kernel, rows, columns), out_shape=j...  11.6 us
    unnamed x64, local copies, waits for them, and re-layouts  9.66 us
    pallas_call x1, Pallas kernels, inject_and_project(): pl.pallas_call(functools.partial(inject_kernel, groups), out_shape=(jax.S...  8.94 us
  transfers between devices with their start and end apart: 25, of which 12 were waited for; matrix products, arithmetic and copies ran while one was open for 7% of the time, Pallas kernels for 19%

profile of v3, /device:TPU:88, one launch (start us, length us, event | category | flops | bytes accessed | tf_op | source)
XLA Modules:
  0.0 187.5 jit_solution(8280455912518087905)
XLA Ops:
  8.9 16.3 %all_to_all.12 = bf16[32,2,2560]{2,1,0:T(2,128)(2,1)S(1)} all-to-all(bf16[32,2,2560]{2,1,0:T(2,128)(2,1)S(1)} %all_to_all.8), channel_id=1, replica_groups=mesh['enc'=4,'ctx'=32,'tp'=2] {'ctx'}, dimensions={0} | all-to-all | bytes 655360 | tf_op jit(solution)/shard_map/all_to_all | solution.py:466
  28.4 1.3 collective-permute-start.4
  30.8 3.5 %collective-permute-done.refs_1_ = bf16[1,160,768]{2,1,0:T(8,128)(2,1)S(1)} collective-permute-done((bf16[1,160,768]{2,1,0:T(8,128)(2,1)S(1)}, bf16[1,160,768]{2,1,0:T(8,128)(2,1)S(1)}, u32[]{:S(2)}, u32[]{:S(2)}) %collective-permute-start) | collective-permute-done | bytes 245792 | tf_op jit(solution)/shard_map/ppermute | solution.py:89
  35.0 1.9 join.6.refs_0_
  36.9 1.2 collective-permute-start.1
  38.0 2.2 %collective-permute-start.2 = (bf16[2,160,768]{2,1,0:T(8,128)(2,1)}, bf16[2,160,768]{2,1,0:T(8,128)(2,1)S(1)}, u32[]{:S(2)}, u32[]{:S(2)}) collective-permute-start(bf16[2,160,768]{2,1,0:T(8,128)(2,1)} %join.6.refs_0_), channel_id=1, source_target_pairs={{0,6},{1,49},{2,0},{3,51},{4,2},{5,53},{6,4},{7,55},{8,14},{9,57},... | collective-permute-start | bytes 1474568 | tf_op jit(solution)/shard_map/ppermute | solution.py:49
  44.3 8.1 %collective-permute-done.1.refs_1_ = bf16[2,160,768]{2,1,0:T(8,128)(2,1)S(1)} collective-permute-done((bf16[2,160,768]{2,1,0:T(8,128)(2,1)}, bf16[2,160,768]{2,1,0:T(8,128)(2,1)S(1)}, u32[]{:S(2)}, u32[]{:S(2)}) %collective-permute-start.1) | collective-permute-done | bytes 491552 | tf_op jit(solution)/shard_map/ppermute | solution.py:49
  54.2 2.0 %join.7.refs_1_ = bf16[8,160,256]{2,1,0:T(8,128)(2,1)} custom-call(bf16[2,160,768]{2,1,0:T(8,128)(2,1)} %join.6.refs_0_, bf16[2,160,768]{2,1,0:T(8,128)(2,1)} %copy-done.13, bf16[2,160,768]{2,1,0:T(8,128)(2,1)} %copy-done.14, bf16[2,160,768]{2,1,0:T(8,128)(2,1)} %copy-done.15, f32[256,128]{1,0:T(8,128)} %pad_maximum_fusion.4.refs_4_.cos_ref, ...), custom_call_target="tpu_custom_call" | custom-call | bytes 1310720 | tf_op jit(solution)/shard_map/join/pallas_call | solution.py:74
  56.3 2.2 %collective-permute-start.5 = (bf16[8,160,256]{2,1,0:T(8,128)(2,1)}, bf16[8,160,256]{2,1,0:T(8,128)(2,1)S(1)}, u32[]{:S(2)}, u32[]{:S(2)}) collective-permute-start(bf16[8,160,256]{2,1,0:T(8,128)(2,1)} %join.7.refs_1_), channel_id=1, source_target_pairs={{0,16},{1,3},{2,18},{3,5},{4,20},{5,7},{6,22},{7,1},{8,24},{9,11},... | collective-permute-start | bytes 1966088 | tf_op jit(solution)/shard_map/ppermute | solution.py:49
  58.5 2.1 %collective-permute-start.7 = (bf16[8,160,256]{2,1,0:T(8,128)(2,1)}, bf16[8,160,256]{2,1,0:T(8,128)(2,1)S(1)}, u32[]{:S(2)}, u32[]{:S(2)}) collective-permute-start(bf16[8,160,256]{2,1,0:T(8,128)(2,1)} %join.7.refs_1_), channel_id=1, source_target_pairs={{0,32},{1,5},{2,34},{3,7},{4,36},{5,1},{6,38},{7,3},{8,40},{9,13},... | collective-permute-start | bytes 1966088 | tf_op jit(solution)/shard_map/ppermute | solution.py:49
  60.5 1.9 %join.8.refs_0_ = bf16[4,160,512]{2,1,0:T(8,128)(2,1)} custom-call(bf16[2,160,768]{2,1,0:T(8,128)(2,1)} %join.6.refs_0_, bf16[2,160,768]{2,1,0:T(8,128)(2,1)} %copy-done.13), custom_call_target="tpu_custom_call" | custom-call | bytes 1310720 | tf_op jit(solution)/shard_map/join/pallas_call | solution.py:74
  62.5 1.9 %join.9.refs_1_ = bf16[4,160,512]{2,1,0:T(8,128)(2,1)} custom-call(bf16[2,160,768]{2,1,0:T(8,128)(2,1)} %copy-done.14, bf16[2,160,768]{2,1,0:T(8,128)(2,1)} %copy-done.15), custom_call_target="tpu_custom_call" | custom-call | bytes 1310720 | tf_op jit(solution)/shard_map/join/pallas_call | solution.py:74
  64.4 9.5 %collective-permute-done.5.refs_2_ = bf16[8,160,256]{2,1,0:T(8,128)(2,1)S(1)} collective-permute-done((bf16[8,160,256]{2,1,0:T(8,128)(2,1)}, bf16[8,160,256]{2,1,0:T(8,128)(2,1)S(1)}, u32[]{:S(2)}, u32[]{:S(2)}) %collective-permute-start.5) | collective-permute-done | bytes 655392 | tf_op jit(solution)/shard_map/ppermute | solution.py:49
  73.9 3.6 %collective-permute-done.6.refs_3_ = bf16[8,160,256]{2,1,0:T(8,128)(2,1)S(1)} collective-permute-done((bf16[8,160,256]{2,1,0:T(8,128)(2,1)}, bf16[8,160,256]{2,1,0:T(8,128)(2,1)S(1)}, u32[]{:S(2)}, u32[]{:S(2)}) %collective-permute-start.6) | collective-permute-done | bytes 655392 | tf_op jit(solution)/shard_map/ppermute | solution.py:49
  79.2 3.2 %collective-permute-start.11 = (bf16[4,160,512]{2,1,0:T(8,128)(2,1)}, bf16[4,160,512]{2,1,0:T(8,128)(2,1)S(1)}, u32[]{:S(2)}, u32[]{:S(2)}) collective-permute-start(bf16[4,160,512]{2,1,0:T(8,128)(2,1)} %get-tuple-element.13.refs_2_.refs_3_), channel_id=1, source_target_pairs={{0,16},{1,3},{2,18},{3,5},{4,20},{5,7},{6,22},{7,1},{8,24},{9,11},... | collective-permute-start | bytes 1966088 | tf_op jit(solution)/shard_map/ppermute | solution.py:49
  82.5 2.0 %collective-permute-start.12 = (bf16[4,160,512]{2,1,0:T(8,128)(2,1)}, bf16[4,160,512]{2,1,0:T(8,128)(2,1)S(1)}, u32[]{:S(2)}, u32[]{:S(2)}) collective-permute-start(bf16[4,160,512]{2,1,0:T(8,128)(2,1)} %get-tuple-element.11.refs_5_.refs_1_.refs_2_), channel_id=1, source_target_pairs={{0,48},{1,7},{2,50},{3,1},{4,52},{5,3},{6,54},{7,5},{8,56},{9,15},... | collective-permute-start | bytes 1966088 | tf_op jit(solution)/shard_map/ppermute | solution.py:49
  85.1 8.9 %inject_and_project.1 = (bf16[256,5120]{1,0:T(8,128)(2,1)}, bf16[256,256]{1,0:T(8,128)(2,1)}) custom-call(s32[32]{0:T(128)} %fusion.13.order_ref, s32[1,256]{1,0:T(1,128)} %sub.68.refs_8_.rows_ref, bf16[256,5120]{1,0:T(8,128)(2,1)} %hidden_ref.1, f32[1,5120]{1,0:T(1,128)} %bitcast.27, f32[1,128]{1,0:T(1,128)} %bitcast.34, ...), custom_call_target="tpu_custom_call" | custom-call | flops 1342177280 | bytes 7864320 | tf_op jit(solution)/shard_map/inject_and_project/pallas_call | solution.py:208
  94.9 2.5 %constant_dynamic-slice_fusion.refs_0_ = bf16[256,2560]{1,0:T(8,128)(2,1)} fusion(bf16[256,5120]{1,0:T(8,128)(2,1)} %get-tuple-element.12.refs_0_, s32[]{:T(128)S(6)} %select_n.167), kind=kLoop, calls=%fused_computation.55 | loop fusion | bytes 2621444 | tf_op jit(solution)/shard_map/dynamic_slice | solution.py:493
  100.0 1.7 join.10.refs_2_.refs_1_.refs_0_
  102.6 3.6 %collective-permute-start.13 = (bf16[4,160,512]{2,1,0:T(8,128)(2,1)}, bf16[4,160,512]{2,1,0:T(8,128)(2,1)S(1)}, u32[]{:S(2)}, u32[]{:S(2)}) collective-permute-start(bf16[4,160,512]{2,1,0:T(8,128)(2,1)} %get-tuple-element.15.refs_3_.refs_4_), channel_id=1, source_target_pairs={{0,16},{1,3},{2,18},{3,5},{4,20},{5,7},{6,22},{7,1},{8,24},{9,11},... | collective-permute-start | bytes 1966088 | tf_op jit(solution)/shard_map/ppermute | solution.py:49
  106.4 3.0 %collective-permute-start.17 = (bf16[2,256,256]{2,1,0:T(8,128)(2,1)S(1)}, bf16[2,256,256]{2,1,0:T(8,128)(2,1)S(1)}, u32[]{:S(2)}, u32[]{:S(2)}) collective-permute-start(bf16[2,256,256]{2,1,0:T(8,128)(2,1)S(1)} %copy-done.9), channel_id=1, source_target_pairs={{0,6},{1,49},{2,0},{3,51},{4,2},{5,53},{6,4},{7,55},{8,14},{9,57},... | collective-permute-start | bytes 786440 | tf_op jit(solution)/shard_map/ppermute | solution.py:49
  109.4 4.3 %collective-permute-done.16.refs_1_ = bf16[2,256,256]{2,1,0:T(8,128)(2,1)S(1)} collective-permute-done((bf16[2,256,256]{2,1,0:T(8,128)(2,1)S(1)}, bf16[2,256,256]{2,1,0:T(8,128)(2,1)S(1)}, u32[]{:S(2)}, u32[]{:S(2)}) %collective-permute-start.16) | collective-permute-done | bytes 262176 | tf_op jit(solution)/shard_map/ppermute | solution.py:49
  114.6 7.0 %collective-permute-done.18.refs_3_ = bf16[2,256,256]{2,1,0:T(8,128)(2,1)S(1)} collective-permute-done((bf16[2,256,256]{2,1,0:T(8,128)(2,1)S(1)}, bf16[2,256,256]{2,1,0:T(8,128)(2,1)S(1)}, u32[]{:S(2)}, u32[]{:S(2)}) %collective-permute-start.18) | collective-permute-done | bytes 262176 | tf_op jit(solution)/shard_map/ppermute | solution.py:49
  123.5 2.2 %join.11.refs_1_.refs_0_ = bf16[8,256,256]{2,1,0:T(8,128)(2,1)} custom-call(bf16[2,256,256]{2,1,0:T(8,128)(2,1)} %join.10.refs_2_.refs_1_.refs_0_, bf16[2,256,256]{2,1,0:T(8,128)(2,1)} %copy-done.18, bf16[2,256,256]{2,1,0:T(8,128)(2,1)} %copy-done.19, bf16[2,256,256]{2,1,0:T(8,128)(2,1)} %copy-done.20, bf16[4,160,512]{2,1,0:T(8,128)(2,1)} %copy-done.5, ...), custom_call_target="tpu_custom_call" | custom-call | bytes 2097152 | tf_op jit(solution)/shard_map/join/pallas_call | solution.py:74
  125.7 2.9 %collective-permute-done.15.refs_0_ = bf16[256,2560]{1,0:T(8,128)(2,1)S(1)} collective-permute-done((bf16[256,2560]{1,0:T(8,128)(2,1)}, bf16[256,2560]{1,0:T(8,128)(2,1)S(1)}, u32[]{:S(2)}, u32[]{:S(2)}) %collective-permute-start.15) | collective-permute-done | bytes 1310752 | tf_op jit(solution)/shard_map/ppermute | solution.py:89
  128.5 1.1 copy-done.7
  130.6 1.1 collective-permute-start.22
  134.0 8.1 %project.3 = bf16[256,512]{1,0:T(8,128)(2,1)} custom-call(s32[32]{0:T(128)} %fusion.13.order_ref, s32[2]{0:T(128)} %pad_add_fusion.places_ref, f32[1,128]{1,0:T(1,128)} %bitcast.32, f32[256,128]{1,0:T(8,128)} %pad_maximum_fusion.6.refs_6_.cos_ref, f32[256,128]{1,0:T(8,128)} %pad_maximum_fusion.7.refs_7_.sin_ref, bf16[256,2560]{1,0:T(8,128)(2,1)} %hold.7.refs_0_, ...), custom_call_target="tpu_custom_call" | custom-call | flops 1342177280 | bytes 7864320 | tf_op jit(solution)/shard_map/project/pallas_call | solution.py:259
  142.0 1.1 collective-permute-start.20
  143.2 1.1 convert_reduce_fusion
  149.4 8.0 %project.2.near_ref = bf16[256,512]{1,0:T(8,128)(2,1)} custom-call(s32[32]{0:T(128)} %fusion.13.order_ref, s32[1]{0:T(128)} %constant.189.clone.1.places_ref, f32[1,128]{1,0:T(1,128)} %bitcast.33, f32[256,128]{1,0:T(8,128)} %pad_maximum_fusion.4.refs_4_.cos_ref, f32[256,128]{1,0:T(8,128)} %pad_maximum_fusion.5.refs_5_.sin_ref, ...), custom_call_target="tpu_custom_call" | custom-call | flops 1342177280 | bytes 7864320 | tf_op jit(solution)/shard_map/project/pallas_call | solution.py:259
  158.6 22.0 %attend.1 = bf16[256,1024]{1,0:T(8,128)(2,1)} custom-call(s32[32]{0:T(128)} %fusion.13.order_ref, s32[7]{0:T(128)} %stack.37.plan_ref, bf16[256,512]{1,0:T(8,128)(2,1)} %project.2.near_ref, bf16[256,512]{1,0:T(8,128)(2,1)} %copy-done.31, s32[256,1]{1,0:T(8,128)} %copy.37.start_ref, bf16[8,256,256]{2,1,0:T(8,128)(2,1)} %join.11.refs_1_.refs_0_, ...), custom_call_target="tpu_custom_call" | custom-call | flops 4294967296 | bytes 5242880 | tf_op jit(solution)/shard_map/attend/pallas_call | solution.py:363
  (137 shorter events, 29.1 us)
Async XLA Ops:
  6.5 23.2 %copy-start.26 = (s32[4096]{0:T(1024)S(1)}, s32[4096]{0:T(1024)}, u32[]{:S(2)}) copy-start(s32[4096]{0:T(1024)} %param.16) | copy-start | bytes 49156
  6.5 19.6 %copy-start.23 = (bf16[160,128]{1,0:T(8,128)(2,1)S(1)}, bf16[160,128]{1,0:T(8,128)(2,1)}, u32[]{:S(2)}) copy-start(bf16[160,128]{1,0:T(8,128)(2,1)} %param.22) | copy-start | bytes 122884
  6.5 19.6 %copy-start.24 = (bf16[160,128]{1,0:T(8,128)(2,1)S(1)}, bf16[160,128]{1,0:T(8,128)(2,1)}, u32[]{:S(2)}) copy-start(bf16[160,128]{1,0:T(8,128)(2,1)} %param.21) | copy-start | bytes 122884
  6.5 21.2 %copy-start.27 = (s32[3,256]{1,0:T(4,128)S(1)}, s32[3,256]{1,0:T(4,128)}, u32[]{:S(2)}) copy-start(s32[3,256]{1,0:T(4,128)} %param.17) | copy-start | bytes 9220
  6.6 78.5 %all-gather.2.cloned.1.call-start = ((), (), s32[]{:S(2)}) async-start(), calls=%async_computation.1 | async-start | bytes 2949120 | tf_op jit(solution)/shard_map/all_gather | solution.py:467
  26.9 7.4 %collective-permute-start = (bf16[1,160,768]{2,1,0:T(8,128)(2,1)S(1)}, bf16[1,160,768]{2,1,0:T(8,128)(2,1)S(1)}, u32[]{:S(2)}, u32[]{:S(2)}) collective-permute-start(bf16[1,160,768]{2,1,0:T(8,128)(2,1)S(1)} %get-tuple-element.23), channel_id=1, source_target_pairs={{0,8},{1,9},{2,10},{3,11},{4,12},{5,13},{6,14},{7,15},{8,0},{9,1},... | collective-permute-start | bytes 737288 | tf_op jit(solution)/shard_map/ppermute | solution.py:89
  28.4 14.0 %collective-permute-start.4 = (f32[256,64]{1,0:T(8,128)S(1)}, f32[256,64]{1,0:T(8,128)S(1)}, u32[]{:S(2)}, u32[]{:S(2)}) collective-permute-start(f32[256,64]{1,0:T(8,128)S(1)} %get-tuple-element.25), channel_id=1, source_target_pairs={{0,8},{1,9},{2,10},{3,11},{4,12},{5,13},{6,14},{7,15},{8,0},{9,1},... | collective-permute-start | bytes 196616 | tf_op jit(solution)/shard_map/ppermute | solution.py:89
  36.9 15.6 %collective-permute-start.1 = (bf16[2,160,768]{2,1,0:T(8,128)(2,1)}, bf16[2,160,768]{2,1,0:T(8,128)(2,1)S(1)}, u32[]{:S(2)}, u32[]{:S(2)}) collective-permute-start(bf16[2,160,768]{2,1,0:T(8,128)(2,1)} %join.6.refs_0_), channel_id=1, source_target_pairs={{0,2},{1,17},{2,4},{3,19},{4,6},{5,21},{6,0},{7,23},{8,10},{9,25},... | collective-permute-start | bytes 1474568 | tf_op jit(solution)/shard_map/ppermute | solution.py:49
  38.0 14.4 %collective-permute-start.2 = (bf16[2,160,768]{2,1,0:T(8,128)(2,1)}, bf16[2,160,768]{2,1,0:T(8,128)(2,1)S(1)}, u32[]{:S(2)}, u32[]{:S(2)}) collective-permute-start(bf16[2,160,768]{2,1,0:T(8,128)(2,1)} %join.6.refs_0_), channel_id=1, source_target_pairs={{0,6},{1,49},{2,0},{3,51},{4,2},{5,53},{6,4},{7,55},{8,14},{9,57},... | collective-permute-start | bytes 1474568 | tf_op jit(solution)/shard_map/ppermute | solution.py:49
  40.2 12.3 %collective-permute-start.3 = (bf16[2,160,768]{2,1,0:T(8,128)(2,1)}, bf16[2,160,768]{2,1,0:T(8,128)(2,1)S(1)}, u32[]{:S(2)}, u32[]{:S(2)}) collective-permute-start(bf16[2,160,768]{2,1,0:T(8,128)(2,1)} %join.6.refs_0_), channel_id=1, source_target_pairs={{0,4},{1,33},{2,6},{3,35},{4,0},{5,37},{6,2},{7,39},{8,12},{9,41},... | collective-permute-start | bytes 1474568 | tf_op jit(solution)/shard_map/ppermute | solution.py:49
  56.3 17.6 %collective-permute-start.5 = (bf16[8,160,256]{2,1,0:T(8,128)(2,1)}, bf16[8,160,256]{2,1,0:T(8,128)(2,1)S(1)}, u32[]{:S(2)}, u32[]{:S(2)}) collective-permute-start(bf16[8,160,256]{2,1,0:T(8,128)(2,1)} %join.7.refs_1_), channel_id=1, source_target_pairs={{0,16},{1,3},{2,18},{3,5},{4,20},{5,7},{6,22},{7,1},{8,24},{9,11},... | collective-permute-start | bytes 1966088 | tf_op jit(solution)/shard_map/ppermute | solution.py:49
  58.5 19.0 %collective-permute-start.6 = (bf16[8,160,256]{2,1,0:T(8,128)(2,1)}, bf16[8,160,256]{2,1,0:T(8,128)(2,1)S(1)}, u32[]{:S(2)}, u32[]{:S(2)}) collective-permute-start(bf16[8,160,256]{2,1,0:T(8,128)(2,1)} %join.7.refs_1_), channel_id=1, source_target_pairs={{0,48},{1,7},{2,50},{3,1},{4,52},{5,3},{6,54},{7,5},{8,56},{9,15},... | collective-permute-start | bytes 1966088 | tf_op jit(solution)/shard_map/ppermute | solution.py:49
  58.5 19.0 %collective-permute-start.7 = (bf16[8,160,256]{2,1,0:T(8,128)(2,1)}, bf16[8,160,256]{2,1,0:T(8,128)(2,1)S(1)}, u32[]{:S(2)}, u32[]{:S(2)}) collective-permute-start(bf16[8,160,256]{2,1,0:T(8,128)(2,1)} %join.7.refs_1_), channel_id=1, source_target_pairs={{0,32},{1,5},{2,34},{3,7},{4,36},{5,1},{6,38},{7,3},{8,40},{9,13},... | collective-permute-start | bytes 1966088 | tf_op jit(solution)/shard_map/ppermute | solution.py:49
  62.4 22.0 %copy-start.28 = (s32[32]{0:T(128)S(1)}, s32[32]{0:T(128)}, u32[]{:S(2)}) copy-start(s32[32]{0:T(128)} %constant.203.clone) | copy-start | bytes 388
  62.5 22.0 %copy-start.29 = (s32[32]{0:T(128)S(1)}, s32[32]{0:T(128)}, u32[]{:S(2)}) copy-start(s32[32]{0:T(128)} %constant.202.clone) | copy-start | bytes 388
  62.5 22.0 %copy-start.30 = (s32[32]{0:T(128)S(1)}, s32[32]{0:T(128)}, u32[]{:S(2)}) copy-start(s32[32]{0:T(128)} %constant.201.clone) | copy-start | bytes 388
  79.2 18.7 %collective-permute-start.9 = (bf16[4,160,512]{2,1,0:T(8,128)(2,1)}, bf16[4,160,512]{2,1,0:T(8,128)(2,1)S(1)}, u32[]{:S(2)}, u32[]{:S(2)}) collective-permute-start(bf16[4,160,512]{2,1,0:T(8,128)(2,1)} %get-tuple-element.13.refs_2_.refs_3_), channel_id=1, source_target_pairs={{0,48},{1,7},{2,50},{3,1},{4,52},{5,3},{6,54},{7,5},{8,56},{9,15},... | collective-permute-start | bytes 1966088 | tf_op jit(solution)/shard_map/ppermute | solution.py:49
  79.2 18.7 %collective-permute-start.11 = (bf16[4,160,512]{2,1,0:T(8,128)(2,1)}, bf16[4,160,512]{2,1,0:T(8,128)(2,1)S(1)}, u32[]{:S(2)}, u32[]{:S(2)}) collective-permute-start(bf16[4,160,512]{2,1,0:T(8,128)(2,1)} %get-tuple-element.13.refs_2_.refs_3_), channel_id=1, source_target_pairs={{0,16},{1,3},{2,18},{3,5},{4,20},{5,7},{6,22},{7,1},{8,24},{9,11},... | collective-permute-start | bytes 1966088 | tf_op jit(solution)/shard_map/ppermute | solution.py:49
  82.5 15.4 %collective-permute-start.8 = (bf16[4,160,512]{2,1,0:T(8,128)(2,1)}, bf16[4,160,512]{2,1,0:T(8,128)(2,1)S(1)}, u32[]{:S(2)}, u32[]{:S(2)}) collective-permute-start(bf16[4,160,512]{2,1,0:T(8,128)(2,1)} %get-tuple-element.11.refs_5_.refs_1_.refs_2_), channel_id=1, source_target_pairs={{0,16},{1,3},{2,18},{3,5},{4,20},{5,7},{6,22},{7,1},{8,24},{9,11},... | collective-permute-start | bytes 1966088 | tf_op jit(solution)/shard_map/ppermute | solution.py:49
  82.5 15.8 %collective-permute-start.12 = (bf16[4,160,512]{2,1,0:T(8,128)(2,1)}, bf16[4,160,512]{2,1,0:T(8,128)(2,1)S(1)}, u32[]{:S(2)}, u32[]{:S(2)}) collective-permute-start(bf16[4,160,512]{2,1,0:T(8,128)(2,1)} %get-tuple-element.11.refs_5_.refs_1_.refs_2_), channel_id=1, source_target_pairs={{0,48},{1,7},{2,50},{3,1},{4,52},{5,3},{6,54},{7,5},{8,56},{9,15},... | collective-permute-start | bytes 1966088 | tf_op jit(solution)/shard_map/ppermute | solution.py:49
  94.1 5.2 %collective-permute-start.10 = (bf16[1,256,256]{2,1,0:T(8,128)(2,1)}, bf16[1,256,256]{2,1,0:T(8,128)(2,1)S(1)}, u32[]{:S(2)}, u32[]{:S(2)}) collective-permute-start(bf16[1,256,256]{2,1,0:T(8,128)(2,1)} %bitcast.25), channel_id=1, source_target_pairs={{0,8},{1,9},{2,10},{3,11},{4,12},{5,13},{6,14},{7,15},{8,0},{9,1},... | collective-permute-start | bytes 393224 | tf_op jit(solution)/shard_map/ppermute | solution.py:89
  101.7 26.8 %collective-permute-start.15 = (bf16[256,2560]{1,0:T(8,128)(2,1)}, bf16[256,2560]{1,0:T(8,128)(2,1)S(1)}, u32[]{:S(2)}, u32[]{:S(2)}) collective-permute-start(bf16[256,2560]{1,0:T(8,128)(2,1)} %hold.6), channel_id=1, source_target_pairs={{0,8},{1,9},{2,10},{3,11},{4,12},{5,13},{6,14},{7,15},{8,0},{9,1},... | collective-permute-start | bytes 3932168 | tf_op jit(solution)/shard_map/ppermute | solution.py:89
  102.6 19.1 %collective-permute-start.13 = (bf16[4,160,512]{2,1,0:T(8,128)(2,1)}, bf16[4,160,512]{2,1,0:T(8,128)(2,1)S(1)}, u32[]{:S(2)}, u32[]{:S(2)}) collective-permute-start(bf16[4,160,512]{2,1,0:T(8,128)(2,1)} %get-tuple-element.15.refs_3_.refs_4_), channel_id=1, source_target_pairs={{0,16},{1,3},{2,18},{3,5},{4,20},{5,7},{6,22},{7,1},{8,24},{9,11},... | collective-permute-start | bytes 1966088 | tf_op jit(solution)/shard_map/ppermute | solution.py:49
  106.2 15.5 %collective-permute-start.14 = (bf16[4,160,512]{2,1,0:T(8,128)(2,1)}, bf16[4,160,512]{2,1,0:T(8,128)(2,1)S(1)}, u32[]{:S(2)}, u32[]{:S(2)}) collective-permute-start(bf16[4,160,512]{2,1,0:T(8,128)(2,1)} %get-tuple-element.16.refs_6_.refs_7_), channel_id=1, source_target_pairs={{0,48},{1,7},{2,50},{3,1},{4,52},{5,3},{6,54},{7,5},{8,56},{9,15},... | collective-permute-start | bytes 1966088 | tf_op jit(solution)/shard_map/ppermute | solution.py:49
  106.2 7.6 %collective-permute-start.16 = (bf16[2,256,256]{2,1,0:T(8,128)(2,1)S(1)}, bf16[2,256,256]{2,1,0:T(8,128)(2,1)S(1)}, u32[]{:S(2)}, u32[]{:S(2)}) collective-permute-start(bf16[2,256,256]{2,1,0:T(8,128)(2,1)S(1)} %copy-done.9), channel_id=1, source_target_pairs={{0,2},{1,17},{2,4},{3,19},{4,6},{5,21},{6,0},{7,23},{8,10},{9,25},... | collective-permute-start | bytes 786440 | tf_op jit(solution)/shard_map/ppermute | solution.py:49
  106.4 8.2 %collective-permute-start.17 = (bf16[2,256,256]{2,1,0:T(8,128)(2,1)S(1)}, bf16[2,256,256]{2,1,0:T(8,128)(2,1)S(1)}, u32[]{:S(2)}, u32[]{:S(2)}) collective-permute-start(bf16[2,256,256]{2,1,0:T(8,128)(2,1)S(1)} %copy-done.9), channel_id=1, source_target_pairs={{0,6},{1,49},{2,0},{3,51},{4,2},{5,53},{6,4},{7,55},{8,14},{9,57},... | collective-permute-start | bytes 786440 | tf_op jit(solution)/shard_map/ppermute | solution.py:49
  113.8 7.9 %collective-permute-start.18 = (bf16[2,256,256]{2,1,0:T(8,128)(2,1)S(1)}, bf16[2,256,256]{2,1,0:T(8,128)(2,1)S(1)}, u32[]{:S(2)}, u32[]{:S(2)}) collective-permute-start(bf16[2,256,256]{2,1,0:T(8,128)(2,1)S(1)} %copy-done.9), channel_id=1, source_target_pairs={{0,4},{1,33},{2,6},{3,35},{4,0},{5,37},{6,2},{7,39},{8,12},{9,41},... | collective-permute-start | bytes 786440 | tf_op jit(solution)/shard_map/ppermute | solution.py:49
  129.7 3.2 %collective-permute-start.19 = (bf16[256,2560]{1,0:T(8,128)(2,1)}, bf16[256,2560]{1,0:T(8,128)(2,1)S(1)}, u32[]{:S(2)}, u32[]{:S(2)}) collective-permute-start(bf16[256,2560]{1,0:T(8,128)(2,1)} %hold.7.refs_0_), channel_id=1, source_target_pairs={{0,1},{1,0},{2,3},{3,2},{4,5},{5,4},{6,7},{7,6},{8,9},{9,8},{10,11... | collective-permute-start | bytes 3932168 | tf_op jit(solution)/shard_map/ppermute | solution.py:497
  129.7 27.8 %collective-permute-start.21 = (bf16[8,256,256]{2,1,0:T(8,128)(2,1)S(1)}, bf16[8,256,256]{2,1,0:T(8,128)(2,1)}, u32[]{:S(2)}, u32[]{:S(2)}) collective-permute-start(bf16[8,256,256]{2,1,0:T(8,128)(2,1)S(1)} %copy-done.8), channel_id=1, source_target_pairs={{0,16},{1,3},{2,18},{3,5},{4,20},{5,7},{6,22},{7,1},{8,24},{9,11},... | collective-permute-start | bytes 3145736 | tf_op jit(solution)/shard_map/ppermute | solution.py:49
  130.6 27.4 %collective-permute-start.22 = (bf16[8,256,256]{2,1,0:T(8,128)(2,1)S(1)}, bf16[8,256,256]{2,1,0:T(8,128)(2,1)}, u32[]{:S(2)}, u32[]{:S(2)}) collective-permute-start(bf16[8,256,256]{2,1,0:T(8,128)(2,1)S(1)} %copy-done.8), channel_id=1, source_target_pairs={{0,48},{1,7},{2,50},{3,1},{4,52},{5,3},{6,54},{7,5},{8,56},{9,15},... | collective-permute-start | bytes 3145736 | tf_op jit(solution)/shard_map/ppermute | solution.py:49
  131.7 26.3 %collective-permute-start.23 = (bf16[8,256,256]{2,1,0:T(8,128)(2,1)S(1)}, bf16[8,256,256]{2,1,0:T(8,128)(2,1)}, u32[]{:S(2)}, u32[]{:S(2)}) collective-permute-start(bf16[8,256,256]{2,1,0:T(8,128)(2,1)S(1)} %copy-done.8), channel_id=1, source_target_pairs={{0,32},{1,5},{2,34},{3,7},{4,36},{5,1},{6,38},{7,3},{8,40},{9,13},... | collective-permute-start | bytes 3145736 | tf_op jit(solution)/shard_map/ppermute | solution.py:49
  142.0 15.9 %collective-permute-start.20 = (bf16[256,512]{1,0:T(8,128)(2,1)}, bf16[256,512]{1,0:T(8,128)(2,1)S(1)}, u32[]{:S(2)}, u32[]{:S(2)}) collective-permute-start(bf16[256,512]{1,0:T(8,128)(2,1)} %project.3), channel_id=1, source_target_pairs={{0,8},{1,9},{2,10},{3,11},{4,12},{5,13},{6,14},{7,15},{8,0},{9,1},... | collective-permute-start | bytes 786440 | tf_op jit(solution)/shard_map/ppermute | solution.py:89
  (25 other events, 71.1 us)
Sparse Core Ops, SparseCore 0:
  26.2 38.9 all-gather.1
